TPU v7x, 32 devices: a whole 2x2x4 slice. The times are simulated.
32 devices in a mesh: seq: 8 (over z, x), head: 4 (over y, core).
Axes of the slice: x: 2, y: 2, z: 4, core: 2. Of those that a mesh axis runs over, the one named last changes fastest.
Arguments:
- out_grad: bfloat16 [1024, 768], P('seq', 'head'), may hold values from -6 to 6
- expert_of: int32 [1024], P('seq'), may hold values from 0 to 7, as said below
- counts: int32 [8, 8], P(None, 'seq'), may hold values from 0 to 40, as said below
- w_up: bfloat16 [8, 768, 3072], P('seq', None, 'head'), may hold values from -0.21875 to 0.21875
- w_down: bfloat16 [8, 3072, 768], P('seq', 'head'), may hold values from -0.109375 to 0.109375
- pre_act: bfloat16 [2560, 3072], P('seq', 'head'), may hold values from -6 to 6
- queries: bfloat16 [1024, 1024], P('seq', 'head'), may hold values from -6 to 6
- keys: bfloat16 [1024, 1024], P('seq', 'head'), may hold values from -6 to 6
- values: bfloat16 [1024, 1024], P('seq', 'head'), may hold values from -6 to 6
- w_out: bfloat16 [1024, 768], P('head'), may hold values from -0.1875 to 0.1875
Outputs:
- grad_hidden: bfloat16 [1024, 768], P('seq')
- grad_queries: bfloat16 [1024, 1024], P('seq', 'head')
- grad_keys: bfloat16 [1024, 1024], P('seq', 'head')
- grad_values: bfloat16 [1024, 1024], P('seq', 'head')
Inputs may be any that keep to these rules, and one draw needn't show every extreme that they name: `expert_of`: in each aligned block of 128 tokens at most 40 tokens name one expert; one expert, the same for every block, is named by exactly 40 tokens of every block, and every other expert by fewer than 40 tokens of a block. counts[s, e] is the number of tokens of block s that name expert e.
All inputs are finite; a program needn't handle non-finite values.
Results may differ from a plain program's by a relative error of at most 0.014.
Values may be sent and summed in bfloat16 or wider, within the bound.
A program may use at most 64 MiB of HBM per device.

v0:
```python
import math

import jax
import jax.numpy as jnp
from jax import lax
from jax.sharding import PartitionSpec as P


def shards(out_grad, expert_of, counts, w_up, w_down, pre_act, queries, keys, values, w_out):
    experts = lax.axis_size("seq")
    tok_rows = out_grad.shape[0]
    slot_count = pre_act.shape[0]
    capacity = slot_count // experts
    head_dim = queries.shape[1]
    scaling = 1.0 / math.sqrt(head_dim * tok_rows * experts)
    full_rows = lax.all_gather(out_grad, "head", axis=1, tiled=True)
    expert_ids = jnp.arange(experts, dtype=jnp.int32)
    onehot = (expert_of[:, None] == expert_ids[None, :]).astype(jnp.int32)
    token_rank = jnp.sum((jnp.cumsum(onehot, axis=0) - 1) * onehot, axis=1)
    slot_of = expert_of * capacity + token_rank
    token_of_slot = (
        jnp.full((experts * capacity,), tok_rows, jnp.int32)
        .at[slot_of]
        .set(jnp.arange(tok_rows, dtype=jnp.int32))
    )
    arrived = counts[:, 0]
    offsets = jnp.cumsum(arrived) - arrived
    arrived_total = jnp.sum(arrived)
    packed_ids = jnp.arange(slot_count, dtype=jnp.int32)
    source = jnp.sum((offsets[None, :] <= packed_ids[:, None]).astype(jnp.int32), axis=1) - 1
    within = packed_ids - offsets[source]
    packed_live = packed_ids < arrived_total
    flat_pos = jnp.where(packed_live, source * capacity + within, experts * capacity)
    down_local = w_down[0]
    up_local = w_up[0]
    padded = jnp.concatenate(
        [full_rows, jnp.zeros((1, full_rows.shape[1]), full_rows.dtype)], axis=0
    )
    received = lax.all_to_all(
        padded[token_of_slot].reshape(experts, capacity, full_rows.shape[1]),
        "seq",
        split_axis=0,
        concat_axis=0,
        tiled=True,
    )
    flat_rows = received.reshape(experts * capacity, received.shape[2])
    padded = jnp.concatenate(
        [flat_rows, jnp.zeros((1, flat_rows.shape[1]), flat_rows.dtype)], axis=0
    )
    middle = jnp.dot(padded[flat_pos], down_local.T, preferred_element_type=jnp.float32)
    mid_grad = jnp.where(pre_act > 0, middle, jnp.zeros_like(middle)).astype(jnp.bfloat16)
    hidden_part = jnp.dot(mid_grad, up_local.T, preferred_element_type=jnp.float32)
    slot_ids = jnp.arange(experts * capacity, dtype=jnp.int32)
    slot_source = slot_ids // capacity
    slot_rank = slot_ids % capacity
    slot_live = slot_rank < arrived[slot_source]
    slot_pos = jnp.where(slot_live, offsets[slot_source] + slot_rank, slot_count)
    share_packed = lax.psum_scatter(
        hidden_part.astype(jnp.bfloat16), "head", scatter_dimension=1, tiled=True
    )
    share_width = share_packed.shape[1]
    padded_grad = jnp.concatenate(
        [share_packed, jnp.zeros((1, share_packed.shape[1]), jnp.bfloat16)], axis=0
    )
    returned = lax.all_to_all(
        padded_grad[slot_pos].reshape(experts, capacity, share_packed.shape[1]),
        "seq",
        split_axis=0,
        concat_axis=0,
        tiled=True,
    )
    share_grad = returned.reshape(experts * capacity, share_width)[slot_of]
    expert_grad = lax.all_gather(share_grad, "head", axis=1, tiled=True)
    grad_hidden = (full_rows.astype(jnp.float32) + expert_grad.astype(jnp.float32)).astype(
        jnp.bfloat16
    )
    head_grad = jnp.dot(grad_hidden, w_out.T, preferred_element_type=jnp.float32).astype(
        jnp.bfloat16
    )
    query_part = jnp.dot(queries.T, head_grad, preferred_element_type=jnp.float32)
    key_state, query_state = lax.psum(
        (jnp.dot(keys.T, values, preferred_element_type=jnp.float32), query_part), "seq"
    )
    key_round = key_state.astype(jnp.bfloat16)
    query_round = query_state.astype(jnp.bfloat16)
    grad_queries = (
        scaling * jnp.dot(head_grad, key_round.T, preferred_element_type=jnp.float32)
    ).astype(jnp.bfloat16)
    grad_keys = (
        scaling * jnp.dot(values, query_round.T, preferred_element_type=jnp.float32)
    ).astype(jnp.bfloat16)
    grad_values = (scaling * jnp.dot(keys, query_round, preferred_element_type=jnp.float32)).astype(
        jnp.bfloat16
    )
    return (grad_hidden, grad_queries, grad_keys, grad_values)


def solution(mesh):
    return jax.shard_map(
        shards,
        mesh=mesh,
        in_specs=(
            P("seq", "head"),
            P("seq"),
            P(None, "seq"),
            P("seq", None, "head"),
            P("seq", "head", None),
            P("seq", "head"),
            P("seq", "head"),
            P("seq", "head"),
            P("seq", "head"),
            P("head", None),
        ),
        out_specs=(P("seq", None), P("seq", "head"), P("seq", "head"), P("seq", "head")),
        check_vma=False,
    )
```

profile of v0, /device:TPU:0, one launch (start us, length us, event | category | flops | bytes accessed | tf_op | source)
XLA Modules:
  0.0 143.1 jit_solution(9335411832398378792)
XLA Ops:
  7.2 7.2 %all_gather.6 = bf16[128,768]{0,1:T(8,128)(2,1)S(1)} all-gather(bf16[128,192]{0,1:T(8,128)(2,1)} %param.10), channel_id=1, replica_groups=mesh['seq'=8,'head'=4] {'head'}, dimensions={1}, use_global_device_ids=true | all-gather | bytes 245760 | tf_op jit(solution)/shard_map/all_gather | solution.py:16
  14.5 0.7 fusion.16
  15.5 0.8 select_reduce_fusion
  17.0 1.0 scatter_custom_fusion
  18.0 2.6 %gather_fusion = bf16[320,768]{1,0:T(8,128)(2,1)} fusion(bf16[129,768]{1,0:T(8,128)(2,1)S(1)} %concatenate.9, s32[1024]{0:T(1024)S(1)} %pad_clamp_fusion.3), kind=kCustom, calls=%fused_computation | custom fusion | bytes 984320 | tf_op jit(solution)/shard_map/gather | solution.py:40
  20.6 6.0 %all-to-all-start = ((bf16[8,40,768]{2,1,0:T(8,128)(2,1)}), bf16[8,40,768]{2,1,0:T(8,128)(2,1)S(1)}, u32[]{:S(2)}, u32[]{:S(2)}) async-start(bf16[8,40,768]{2,1,0:T(8,128)(2,1)} %bitcast), calls=%async_computation | async-start | bytes 983040 | tf_op jit(solution)/shard_map/all_to_all | solution.py:39
  28.2 4.5 %fusion.19 = (s32[320]{0:T(512)S(1)}, s32[320,1]{0,1:T(1,128)S(1)}, s32[320]{0:T(512)S(1)}) fusion(s32[]{:T(128)} %bitcast.4, s32[]{:T(128)} %bitcast.5, s32[]{:T(128)} %bitcast.6, s32[]{:T(128)} %bitcast.7, s32[]{:T(128)} %bitcast.8, s32[]{:T(128)} %bitcast.10, s32[]{:T(128)} %bitcast.9, s32[320]{0:T(512)S(1)} %get-tuple-element.25, ...), kind=kLoop, calls=%fused_computation.70 | loop fusion | flops 11840 | bytes 6428 | tf_op jit(solution)/shard_map/gather | solution.py:31
  34.1 6.8 %all-to-all-done = bf16[8,40,768]{2,1,0:T(8,128)(2,1)S(1)} async-done(((bf16[8,40,768]{2,1,0:T(8,128)(2,1)}), bf16[8,40,768]{2,1,0:T(8,128)(2,1)S(1)}, u32[]{:S(2)}, u32[]{:S(2)}) %all-to-all-start) | async-done | bytes 491552 | tf_op jit(solution)/shard_map/all_to_all | solution.py:39
  40.9 2.1 %gather_fusion.1 = bf16[320,768]{1,0:T(8,128)(2,1)S(1)} fusion(bf16[321,768]{1,0:T(8,128)(2,1)S(1)} %concatenate.10, s32[1024]{0:T(1024)S(1)} %pad_clamp_fusion.2), kind=kCustom, calls=%fused_computation.1 | custom fusion | bytes 984320 | tf_op jit(solution)/shard_map/gather | solution.py:50
  43.1 3.4 %convolution_convert_fusion = bf16[320,768]{0,1:T(8,128)(2,1)} fusion(bf16[1,768,768]{2,1,0:T(8,128)(2,1)S(1)} %copy-done, bf16[320,768]{1,0:T(8,128)(2,1)S(1)} %gather_fusion.1, bf16[1,768,768]{2,1,0:T(8,128)(2,1)} %param.14, bf16[320,768]{1,0:T(8,128)(2,1)S(1)} %copy-done.6), kind=kOutput, calls=%fused_computation.6 | convolution fusion | flops 755957760 | bytes 3833856 | tf_op jit(solution)/shard_map/dot_general | solution.py:52
  47.2 4.3 %fusion.18 = s32[320]{0:T(512)S(1)} fusion(s32[]{:T(128)} %bitcast.14, s32[]{:T(128)} %bitcast.15, s32[]{:T(128)} %bitcast.16, s32[]{:T(128)} %bitcast.17, s32[]{:T(128)} %bitcast.18, s32[]{:T(128)} %bitcast.20, s32[]{:T(128)} %bitcast.19), kind=kLoop, calls=%fused_computation.69 | loop fusion | flops 7360 | bytes 1308 | tf_op jit(solution)/shard_map/gather | solution.py:56
  51.5 1.3 broadcast_select_fusion
  52.9 14.9 %reduce-scatter.2.cloned.1.call-done = bf16[320,192]{0,1:T(8,128)(2,1)} async-done(((bf16[320,768]{0,1:T(8,128)(2,1)}), bf16[320,192]{0,1:T(8,128)(2,1)}) %reduce-scatter.2.cloned.1.call-update) | async-done | bytes 122896 | tf_op jit(solution)/shard_map/reduce_scatter | solution.py:58
  67.8 1.0 copy.34
  68.9 2.5 %gather_fusion.2 = bf16[320,192]{1,0:T(8,128)(2,1)} fusion(bf16[321,192]{1,0:T(8,128)(2,1)S(1)} %concatenate.11.clone, s32[1024]{0:T(1024)S(1)} %pad_clamp_fusion.1), kind=kCustom, calls=%fused_computation.2 | custom fusion | bytes 247040 | tf_op jit(solution)/shard_map/gather | solution.py:66
  71.4 5.6 %all-to-all-start.1 = ((bf16[8,40,192]{2,1,0:T(8,128)(2,1)}), bf16[8,40,192]{2,1,0:T(8,128)(2,1)S(1)}, u32[]{:S(2)}, u32[]{:S(2)}) async-start(bf16[8,40,192]{2,1,0:T(8,128)(2,1)} %bitcast.21), calls=%async_computation.2 | async-start | bytes 327680 | tf_op jit(solution)/shard_map/all_to_all | solution.py:65
  77.3 7.3 %all-to-all-done.1 = bf16[8,40,192]{2,1,0:T(8,128)(2,1)S(1)} async-done(((bf16[8,40,192]{2,1,0:T(8,128)(2,1)}), bf16[8,40,192]{2,1,0:T(8,128)(2,1)S(1)}, u32[]{:S(2)}, u32[]{:S(2)}) %all-to-all-start.1) | async-done | bytes 122912 | tf_op jit(solution)/shard_map/all_to_all | solution.py:65
  84.6 0.8 gather_fusion.3
  85.6 5.6 %all-gather = bf16[128,768]{0,1:T(8,128)(2,1)S(1)} all-gather(bf16[128,192]{0,1:T(8,128)(2,1)S(1)} %copy.30), channel_id=2, replica_groups=mesh['seq'=8,'head'=4] {'head'}, dimensions={1}, use_global_device_ids=true | all-gather | bytes 245760 | tf_op jit(solution)/shard_map/all_gather | solution.py:73
  91.8 40.9 %all-reduce.5 = (bf16[256,256]{1,0:T(8,128)(2,1)S(1)}, bf16[256,256]{0,1:T(8,128)(2,1)S(1)}) all-reduce(f32[256,256]{1,0:T(8,128)S(1)} %fusion.29, f32[256,256]{0,1:T(8,128)S(1)} %convolution_bitcast_fusion), channel_id=1, replica_groups=mesh['seq'=8,'head'=4] {'seq'}, use_global_device_ids=true, to_apply=%region_7.8 | all-reduce | flops 131072 | bytes 786432 | tf_op jit(solution)/shard_map/psum | solution.py:81
  133.1 0.8 copy.31
  133.9 0.8 fusion.5
  134.8 0.7 copy.32
  135.5 0.7 copy.33
  (46 shorter events, 6.1 us)
Async XLA Ops:
  7.2 35.9 %copy-start = (bf16[1,768,768]{2,1,0:T(8,128)(2,1)S(1)}, bf16[1,768,768]{2,1,0:T(8,128)(2,1)}, u32[]{:S(2)}) copy-start(bf16[1,768,768]{2,1,0:T(8,128)(2,1)} %param.13) | copy-start | bytes 3538948
  18.0 8.7 %copy-start.5 = (s32[8,1]{0,1:T(1,128)S(1)}, s32[8,1]{0,1:T(1,128)}, u32[]{:S(2)}) copy-start(s32[8,1]{0,1:T(1,128)} %param.12) | copy-start | bytes 100
  20.6 20.3 %all-to-all-start = ((bf16[8,40,768]{2,1,0:T(8,128)(2,1)}), bf16[8,40,768]{2,1,0:T(8,128)(2,1)S(1)}, u32[]{:S(2)}, u32[]{:S(2)}) async-start(bf16[8,40,768]{2,1,0:T(8,128)(2,1)} %bitcast), calls=%async_computation | async-start | bytes 983040 | tf_op jit(solution)/shard_map/all_to_all | solution.py:39
  26.6 41.2 %reduce-scatter.2.cloned.1.call-start = ((), (), s32[]{:S(2)}) async-start(), calls=%async_computation.3 | async-start | bytes 737280 | tf_op jit(solution)/shard_map/reduce_scatter | solution.py:58
  40.9 2.2 %copy-start.6 = (bf16[320,768]{1,0:T(8,128)(2,1)S(1)}, bf16[320,768]{1,0:T(8,128)(2,1)}, u32[]{:S(2)}) copy-start(bf16[320,768]{1,0:T(8,128)(2,1)} %param.15) | copy-start | bytes 1474564
  52.9 24.2 %copy-start.2 = (bf16[128,256]{1,0:T(8,128)(2,1)S(1)}, bf16[128,256]{1,0:T(8,128)(2,1)}, u32[]{:S(2)}) copy-start(bf16[128,256]{1,0:T(8,128)(2,1)} %param.18) | copy-start | bytes 196612
  52.9 24.2 %copy-start.3 = (bf16[128,256]{1,0:T(8,128)(2,1)S(1)}, bf16[128,256]{1,0:T(8,128)(2,1)}, u32[]{:S(2)}) copy-start(bf16[128,256]{1,0:T(8,128)(2,1)} %param.17) | copy-start | bytes 196612
  71.4 19.8 %copy-start.1 = (bf16[256,768]{1,0:T(8,128)(2,1)S(1)}, bf16[256,768]{1,0:T(8,128)(2,1)}, u32[]{:S(2)}) copy-start(bf16[256,768]{1,0:T(8,128)(2,1)} %param.19) | copy-start | bytes 1179652
  71.4 13.2 %all-to-all-start.1 = ((bf16[8,40,192]{2,1,0:T(8,128)(2,1)}), bf16[8,40,192]{2,1,0:T(8,128)(2,1)S(1)}, u32[]{:S(2)}, u32[]{:S(2)}) async-start(bf16[8,40,192]{2,1,0:T(8,128)(2,1)} %bitcast.21), calls=%async_computation.2 | async-start | bytes 327680 | tf_op jit(solution)/shard_map/all_to_all | solution.py:65
  77.3 14.3 %copy-start.4 = (bf16[128,256]{1,0:T(8,128)(2,1)S(1)}, bf16[128,256]{1,0:T(8,128)(2,1)}, u32[]{:S(2)}) copy-start(bf16[128,256]{1,0:T(8,128)(2,1)} %param.16) | copy-start | bytes 196612
Sparse Core Ops, SparseCore 0:
  46.6 21.1 reduce-scatter.1
where the time goes:
time: 144 us; the launch traced here: 143 us
  blocking collectives  53.7 us (37%)
  waiting for transfers between devices  29 us (20%)
  other arithmetic  14.9 us (10%)
  between operations  14.3 us (10%)
  local copies, waits for them, and re-layouts  14.1 us (10%)
  starting transfers between devices  11.7 us (8%)
  matrix products  5.32 us (4%)
    psum x1, blocking collectives, shards(): lax.psum((jnp.dot(keys.T, values, preferred_element_type=jnp.float32), qu...  40.9 us
    reduce_scatter x1, waiting for transfers between devices, shards(): lax.psum_scatter(hidden_part.astype(jnp.bfloat16), 'head', scatter_dimens...  14.9 us
    all_to_all x1, waiting for transfers between devices, shards(): lax.all_to_all(padded_grad[slot_pos].reshape(experts, capacity, share_pac...  7.32 us
    all_gather x1, blocking collectives, shards(): full_rows = lax.all_gather(out_grad, 'head', axis=1, tiled=True)  7.21 us
    all_to_all x1, waiting for transfers between devices, shards(): lax.all_to_all(padded[token_of_slot].reshape(experts, capacity, full_rows...  6.83 us
    all_to_all x1, starting transfers between devices, shards(): lax.all_to_all(padded[token_of_slot].reshape(experts, capacity, full_rows...  5.99 us
    gather x3, other arithmetic, shards(): slot_live = slot_rank < arrived[slot_source]  5.69 us
    all_to_all x1, starting transfers between devices, shards(): lax.all_to_all(padded_grad[slot_pos].reshape(experts, capacity, share_pac...  5.65 us
  transfers between devices with their start and end apart: 3, of which 3 were waited for; matrix products, arithmetic and copies ran while one was open for 10% of the time, Pallas kernels for 0%

commit v1 on v0

--- a/solution.py
+++ b/solution.py
@@ -1,9 +1,329 @@
+import functools
 import math
 
 import jax
 import jax.numpy as jnp
 from jax import lax
+from jax.experimental import pallas as pl
+from jax.experimental.pallas import tpu as pltpu
 from jax.sharding import PartitionSpec as P
+
+MESH = pl.DeviceIdType.MESH
+F32 = jnp.float32
+BF16 = jnp.bfloat16
+ROWS = 16
+
+
+def iota(shape, dim):
+    return lax.broadcasted_iota(jnp.int32, shape, dim)
+
+
+def nn(a, b):
+    return jnp.dot(a, b, preferred_element_type=F32)
+
+
+def nt(a, b):
+    return lax.dot_general(a, b, (((1,), (1,)), ((), ())), preferred_element_type=F32)
+
+
+def kernel(
+    n, cap, pad, scaling,
+    og_ref, expert_ref, counts_ref, up_hbm, down_hbm, pre_hbm, q_ref, k_ref, v_ref, wout_hbm,
+    gh_out, gq_out, gk_out, gv_out,
+    up, down, pre, wout, mask, wide, wide_in, xsend, x, hsum, hsend, hrecv, ysend, yrecv,
+    rsend, ret, eg, eg_in, gh, ks_send, ks_recv, ks, qs_send, qs_recv, qs,
+    load_sem, one_send, one_recv, disp_send, disp_recv, ax_send, ax_recv, as_send, as_recv,
+    ret_send, ret_recv, st_send, st_recv,
+):
+    s = lax.axis_index("seq")
+    h = lax.axis_index("head")
+    c = lax.rem(h, 2)
+    y = lax.div(h, 2)
+    sib = (s, h + 1 - 2 * c)
+    far = (s, lax.rem(h + 2, 4))
+    m = n // 2
+    tok, width = og_ref.shape
+    pair = 2 * width
+    rows = m * pad
+    depth = x.shape[2]
+    piece = ks.shape[1]
+    mine = pl.ds(pl.multiple_of(y * pair, 128), pair)
+    other = pl.ds(pl.multiple_of((1 - y) * pair, 128), pair)
+    parity = lax.rem(s + c, 2)
+
+    def send(src, dst, ssem, rsem, to):
+        return pltpu.make_async_remote_copy(
+            src_ref=src, dst_ref=dst, send_sem=ssem, recv_sem=rsem, device_id=to, device_id_type=MESH
+        )
+
+    barrier = pltpu.get_barrier_semaphore()
+    peers = [lax.rem(s + d, n) for d in range(1, n)]
+    for p in peers:
+        pl.semaphore_signal(barrier, inc=1, device_id=(p, h), device_id_type=MESH)
+    for to in (sib, far):
+        pl.semaphore_signal(barrier, inc=1, device_id=to, device_id_type=MESH)
+    loads = [
+        pltpu.make_async_copy(src, dst, load_sem.at[i])
+        for i, (src, dst) in enumerate(
+            ((pre_hbm, pre), (down_hbm.at[0], down), (up_hbm.at[0], up), (wout_hbm, wout))
+        )
+    ]
+    for load in loads:
+        load.start()
+
+    place = (iota((width, pair), 1) == iota((width, pair), 0) + c * width).astype(BF16)
+    wide[...] = nn(og_ref[...], place).astype(BF16)
+
+    pl.semaphore_wait(barrier, n + 1)
+    pending = []
+
+    def start(copy):
+        copy.start()
+        pending.append(copy)
+        return copy
+
+    gather_wide = start(send(wide, wide_in, one_send.at[0], one_recv.at[0], sib))
+
+    e_row = expert_ref[...]
+    eye = iota((tok, tok), 0) == iota((tok, tok), 1)
+    e_col = jnp.sum(jnp.where(eye, e_row, 0), axis=1, keepdims=True)
+    same = (e_col == e_row).astype(jnp.int32)
+    below = iota((tok, tok), 0) < iota((tok, tok), 1)
+    rank_row = jnp.sum(jnp.where(below, same, 0), axis=0, keepdims=True)
+    above = iota((tok, tok), 1) < iota((tok, tok), 0)
+    rank_col = jnp.sum(jnp.where(above, same, 0), axis=1, keepdims=True)
+    live_row = lax.rem(e_row, 2) == parity
+    slot_row = jnp.where(live_row, lax.div(e_row, 2) * pad + rank_row, -1)
+    live_col = lax.rem(e_col, 2) == parity
+    slot_col = jnp.where(live_col, lax.div(e_col, 2) * pad + rank_col, -1)
+    scatter = (iota((rows, tok), 0) == slot_row).astype(BF16)
+    combine = (iota((tok, rows), 1) == slot_col).astype(BF16)
+
+    ks_part = nn(k_ref[...].T, v_ref[...]).astype(BF16)
+    for p in range(n):
+        ks_send[p] = ks_part[p * piece : (p + 1) * piece]
+
+    gather_wide.wait_recv()
+    full = wide[...] + wide_in[...]
+    wide_in[...] = full
+    blocks = nn(scatter, full).astype(BF16)
+    for i in range(m):
+        xsend[i] = blocks[i * pad : (i + 1) * pad]
+    order = [lax.rem(s + c + 2 * j, n) for j in range(m)]
+    for j, p in enumerate(order):
+        if j == 0:
+            @pl.when(c == 1)
+            def _():
+                send(
+                    xsend.at[lax.div(p, 2)], x.at[c * m + lax.div(s, 2), :, mine],
+                    disp_send.at[j], disp_recv.at[lax.div(s, 2)], (p, h),
+                ).start()
+
+            @pl.when(c == 0)
+            def _():
+                x[lax.div(s, 2), :, mine] = xsend[lax.div(s, 2)]
+        else:
+            start(send(
+                xsend.at[lax.div(p, 2)], x.at[c * m + lax.div(s, 2), :, mine],
+                disp_send.at[j], disp_recv.at[lax.div(s, 2)], (p, h),
+            ))
+
+    def state_scatter(k, source, dest):
+        for d, p in enumerate(peers):
+            start(send(source.at[p], dest.at[s], st_send.at[k, d], st_recv.at[k, s], (p, h)))
+        dest[s] = source[s]
+
+    def state_sum(k, dest, total):
+        for p in peers:
+            send(dest.at[p], dest.at[p], st_send.at[k, 0], st_recv.at[k, p], (p, h)).wait_recv()
+        acc = dest[0].astype(F32)
+        for p in range(1, n):
+            acc = acc + dest[p].astype(F32)
+        total[s] = acc.astype(BF16)
+        for d, p in enumerate(peers):
+            start(send(
+                total.at[s], total.at[s], st_send.at[k + 1, d], st_recv.at[k + 1, s], (p, h)
+            ))
+
+    def state_wait(k, total):
+        for p in peers:
+            send(total.at[p], total.at[p], st_send.at[k, 0], st_recv.at[k, p], (p, h)).wait_recv()
+
+    state_scatter(0, ks_send, ks_recv)
+
+    cnt_row = jnp.sum(
+        jnp.where(iota((n, n), 0) == iota((n, n), 1), counts_ref[...], 0), axis=0, keepdims=True
+    )
+    slot = iota((2 * rows, 1), 0)
+    block = lax.div(slot, pad)
+    source = 2 * lax.rem(block, m) + lax.rem(lax.div(block, m) + s, 2)
+    before = iota((2 * rows, n), 1) < source
+    packed = jnp.sum(jnp.where(before, cnt_row, 0), axis=1, keepdims=True) + lax.rem(slot, pad)
+    unpack = (iota((2 * rows, pre.shape[0]), 1) == packed).astype(BF16)
+    loads[0].wait()
+    mask[...] = nn(unpack, pre[...]).astype(BF16)
+
+    for j, p in enumerate(order):
+        i = lax.div(p, 2)
+        spot = x.at[c * m + i, :, mine]
+
+        def arrived():
+            send(spot, spot, disp_send.at[j], disp_recv.at[i], (p, h)).wait_recv()
+
+        if j == 0:
+            pl.when(c == 1)(arrived)
+        else:
+            arrived()
+        start(send(spot, spot, ax_send.at[j], ax_recv.at[j], far))
+        start(send(spot, spot, as_send.at[j], as_recv.at[j], sib))
+    for j, p in enumerate(order):
+        spot = x.at[c * m + lax.div(p, 2), :, other]
+        send(spot, spot, ax_send.at[j], ax_recv.at[j], far).wait_recv()
+        start(send(spot, spot, as_send.at[m + j], as_recv.at[m + j], sib))
+
+    loads[1].wait()
+    loads[2].wait()
+
+    def expert(cls):
+        at = pl.ds(cls * m, m)
+        xs = x[at].reshape(rows, depth)
+        middle = nt(xs, down[...])
+        live = mask[pl.ds(pl.multiple_of(cls * rows, ROWS), rows), :]
+        mid = jnp.where(live > 0, middle, 0.0).astype(BF16)
+        return nt(mid, up[...])
+
+    hsum[...] = expert(c)
+    sib_order = [lax.rem(s + 1 - c + 2 * j, n) for j in range(m)]
+    for j, p in enumerate(sib_order):
+        for k, half in ((0, mine), (m, other)):
+            spot = x.at[(1 - c) * m + lax.div(p, 2), :, half]
+            send(spot, spot, as_send.at[k + j], as_recv.at[k + j], sib).wait_recv()
+    hsend[...] = expert(1 - c).astype(BF16)
+    pair_sum = start(send(hsend, hrecv, one_send.at[1], one_recv.at[1], sib))
+    state_sum(0, ks_recv, ks)
+    pair_sum.wait_recv()
+    ysend[...] = (hsum[:, other] + hrecv[:, other].astype(F32)).astype(BF16)
+    far_sum = start(send(ysend, yrecv, one_send.at[2], one_recv.at[2], far))
+    own = hsum[:, mine] + hrecv[:, mine].astype(F32)
+    far_sum.wait_recv()
+    rsend[...] = (own + yrecv[...].astype(F32)).astype(BF16).reshape(m, pad, pair)
+
+    for j, p in enumerate(order):
+        i = lax.div(p, 2)
+        if j == 0:
+            @pl.when(c == 1)
+            def _():
+                send(
+                    rsend.at[i], ret.at[lax.div(s, 2)], ret_send.at[j],
+                    ret_recv.at[lax.div(s, 2)], (p, h),
+                ).start()
+
+            @pl.when(c == 0)
+            def _():
+                ret[lax.div(s, 2)] = rsend[lax.div(s, 2)]
+        else:
+            start(send(
+                rsend.at[i], ret.at[lax.div(s, 2)], ret_send.at[j],
+                ret_recv.at[lax.div(s, 2)], (p, h),
+            ))
+    loads[3].wait()
+    q_t = q_ref[...].T
+    for j, p in enumerate(order):
+        i = lax.div(p, 2)
+
+        def arrived():
+            send(ret.at[i], ret.at[i], ret_send.at[j], ret_recv.at[i], (p, h)).wait_recv()
+
+        if j == 0:
+            pl.when(c == 1)(arrived)
+        else:
+            arrived()
+    share = nn(combine, ret[...].reshape(rows, pair))
+    eg[...] = share.astype(BF16)
+    pair_grad = start(send(eg, eg_in, one_send.at[3], one_recv.at[3], sib))
+    own = wide_in[...].astype(F32) + share
+    pair_grad.wait_recv()
+    gh[:, mine] = (own + eg_in[...].astype(F32)).astype(BF16)
+    spot = gh.at[:, mine]
+    far_grad = start(send(spot, spot, one_send.at[4], one_recv.at[4], far))
+    state_wait(1, ks)
+    spot = gh.at[:, other]
+    send(spot, spot, one_send.at[4], one_recv.at[4], far).wait_recv()
+    hidden = gh[...]
+    head_grad = nt(hidden, wout[...]).astype(BF16)
+    qs_part = nn(q_t, head_grad).astype(BF16)
+    for p in range(n):
+        qs_send[p] = qs_part[p * piece : (p + 1) * piece]
+    state_scatter(2, qs_send, qs_recv)
+    gh_out[...] = hidden
+    dim = n * piece
+    gq_out[...] = (scaling * nt(head_grad, ks[...].reshape(dim, dim))).astype(BF16)
+    state_sum(2, qs_recv, qs)
+    state_wait(3, qs)
+    q_round = qs[...].reshape(dim, dim)
+    gk_out[...] = (scaling * nt(v_ref[...], q_round)).astype(BF16)
+    gv_out[...] = (scaling * nn(k_ref[...], q_round)).astype(BF16)
+
+    for copy in pending:
+        copy.wait_send()
+
+    @pl.when(c == 1)
+    def _():
+        send(xsend.at[0], xsend.at[0], disp_send.at[0], disp_recv.at[0], sib).wait_send()
+        send(rsend.at[0], rsend.at[0], ret_send.at[0], ret_recv.at[0], sib).wait_send()
+
+
+def fused(out_grad, expert_of, counts, w_up, w_down, pre_act, queries, keys, values, w_out):
+    n = lax.axis_size("seq")
+    m = n // 2
+    tok, width = out_grad.shape
+    slots = pre_act.shape[0]
+    cap = slots // n
+    pad = -(-cap // ROWS) * ROWS
+    rows = m * pad
+    depth, hidden = w_up.shape[1:]
+    dim = queries.shape[1]
+    pair = 2 * width
+    piece = dim // n
+    scaling = 1.0 / math.sqrt(dim * tok * n)
+    vmem = pl.BlockSpec(memory_space=pltpu.VMEM)
+    hbm = pl.BlockSpec(memory_space=pl.ANY)
+    dma = pltpu.SemaphoreType.DMA
+
+    def buf(*shape, dtype=BF16):
+        return pltpu.VMEM(shape, dtype)
+
+    state = buf(n, piece, dim)
+    out = jax.ShapeDtypeStruct((tok, dim), BF16)
+    return pl.pallas_call(
+        functools.partial(kernel, n, cap, pad, scaling),
+        out_shape=(jax.ShapeDtypeStruct((tok, depth), BF16), out, out, out),
+        in_specs=[vmem, vmem, vmem, hbm, hbm, hbm, vmem, vmem, vmem, hbm],
+        out_specs=(vmem,) * 4,
+        scratch_shapes=[
+            buf(depth, hidden), buf(hidden, depth), buf(slots, hidden), buf(dim, depth),
+            buf(2 * rows, hidden), buf(tok, pair), buf(tok, pair), buf(m, pad, pair),
+            buf(n, pad, depth), buf(rows, depth, dtype=F32), buf(rows, depth), buf(rows, depth),
+            buf(rows, pair), buf(rows, pair), buf(m, pad, pair), buf(m, pad, pair),
+            buf(tok, pair), buf(tok, pair), buf(tok, depth),
+            state, state, state, state, state, state,
+            dma((4,)), dma((5,)), dma((5,)), dma((m,)), dma((m,)), dma((m,)), dma((m,)),
+            dma((n,)), dma((n,)), dma((m,)), dma((m,)), dma((4, n)), dma((4, n)),
+        ],
+        compiler_params=pltpu.CompilerParams(
+            collective_id=0, has_side_effects=True, vmem_limit_bytes=48 * 1024 * 1024
+        ),
+    )(
+        out_grad, expert_of.reshape(1, tok), counts, w_up, w_down, pre_act,
+        queries, keys, values, w_out,
+    )
+
+
+def step(*arrays):
+    n, heads = lax.axis_size("seq"), lax.axis_size("head")
+    width, dim = arrays[0].shape[1], arrays[6].shape[1]
+    fits = heads == 4 and n % 2 == 0 and dim % (n * ROWS) == 0 and 2 * width % 128 == 0
+    return (fused if fits else shards)(*arrays)
 
 
 def shards(out_grad, expert_of, counts, w_up, w_down, pre_act, queries, keys, values, w_out):
@@ -97,7 +417,7 @@
 
 def solution(mesh):
     return jax.shard_map(
-        shards,
+        step,
         mesh=mesh,
         in_specs=(
             P("seq", "head"),

time: 144 us -> 59.4 us (0.41)
  blocking collectives: 53.7 us -> 0 us
  Pallas kernels: 0 us -> 46.3 us
  waiting for transfers between devices: 29 us -> 0 us
  other arithmetic: 14.9 us -> 0 us
  between operations: 14.3 us -> 0.66 us
  starting transfers between devices: 11.7 us -> 0 us
  matrix products: 5.32 us -> 0 us
  local copies, waits for them, and re-layouts: 14.1 us -> 11.9 us
    pallas_call x0 -> x1, Pallas kernels: none -> 46.3 us  [fused(): pl.pallas_call(functools.partial(kernel, n, cap, pad, scaling), out_shape...]
    psum x1 -> x0, blocking collectives: 40.9 us -> none  [shards(): lax.psum((jnp.dot(keys.T, values, preferred_element_type=jnp.float32), qu...]
    reduce_scatter x1 -> x0, waiting for transfers between devices: 14.9 us -> none  [shards(): lax.psum_scatter(hidden_part.astype(jnp.bfloat16), 'head', scatter_dimens...]
    all_to_all x2 -> x0, waiting for transfers between devices: 14.1 us -> none  [the longest x1 7.32 us: shards(): lax.all_to_all(padded_grad[slot_pos].reshape(experts, capacity, share_pac...]
    all_gather x2 -> x0, blocking collectives: 12.8 us -> none  [the longest x1 7.21 us: shards(): full_rows = lax.all_gather(out_grad, 'head', axis=1, tiled=True)]
    all_to_all x2 -> x0, starting transfers between devices: 11.6 us -> none  [the longest x1 5.99 us: shards(): lax.all_to_all(padded[token_of_slot].reshape(experts, capacity, full_rows...]
    gather x10 -> x0, other arithmetic: 10.8 us -> none  [the longest x3 5.69 us: shards(): slot_live = slot_rank < arrived[slot_source]]
    gather x7 -> x0, local copies, waits for them, and re-layouts: 9.56 us -> none  [the longest x1 2.6 us: shards(): padded[token_of_slot].reshape(experts, capacity, full_rows.shape[1])]
  transfers between devices with their start and end apart: 3 -> 0, of which waited for: 3 -> 0; matrix products, arithmetic and copies ran while one was open for 10% -> 0% of each run, Pallas kernels for 0% -> 0%
where the time goes in v1:
time: 59.4 us; the launch traced here: 58.9 us
  Pallas kernels  46.3 us (78%)
  local copies, waits for them, and re-layouts  11.9 us (20%)
  between operations  0.66 us (1%)
    pallas_call x1, Pallas kernels, fused(): pl.pallas_call(functools.partial(kernel, n, cap, pad, scaling), out_shape...  46.3 us
    unnamed x22, local copies, waits for them, and re-layouts  11.9 us

profile of v1, /device:TPU:0, one launch (start us, length us, event | category | flops | bytes accessed | tf_op | source)
XLA Modules:
  0.0 58.9 jit_solution(6680297781575467041)
XLA Ops:
  0.6 0.7 %copy.15.counts_ref = s32[8,1]{1,0:T(8,128)S(1)} copy(s32[8,1]{0,1:T(1,128)} %param.12) | data formatting | bytes 64 | tf_op args[2]
  1.4 0.9 %copy.14.og_ref = bf16[128,192]{1,0:T(8,128)(2,1)S(1)} copy(bf16[128,192]{0,1:T(8,128)(2,1)} %param.10) | data formatting | bytes 98304 | tf_op args[0]
  2.3 0.0 copy-start
  2.3 1.3 %copy-done = bf16[1,768,768]{2,1,0:T(8,128)(2,1)S(1)} copy-done((bf16[1,768,768]{2,1,0:T(8,128)(2,1)S(1)}, bf16[1,768,768]{2,1,0:T(8,128)(2,1)}, u32[]{:S(2)}) %copy-start) | copy-done | bytes 1179672
  3.5 0.0 copy-start.1
  3.5 1.3 %copy-done.1 = bf16[1,768,768]{2,1,0:T(8,128)(2,1)S(1)} copy-done((bf16[1,768,768]{2,1,0:T(8,128)(2,1)S(1)}, bf16[1,768,768]{2,1,0:T(8,128)(2,1)}, u32[]{:S(2)}) %copy-start.1) | copy-done | bytes 1179672
  4.8 0.0 copy-start.2
  4.8 1.0 %copy-done.2 = bf16[320,768]{1,0:T(8,128)(2,1)S(1)} copy-done((bf16[320,768]{1,0:T(8,128)(2,1)S(1)}, bf16[320,768]{1,0:T(8,128)(2,1)}, u32[]{:S(2)}) %copy-start.2) | copy-done | bytes 491544
  5.8 0.0 copy-start.3
  5.8 1.0 %copy-done.3 = bf16[256,768]{1,0:T(8,128)(2,1)S(1)} copy-done((bf16[256,768]{1,0:T(8,128)(2,1)S(1)}, bf16[256,768]{1,0:T(8,128)(2,1)}, u32[]{:S(2)}) %copy-start.3) | copy-done | bytes 393240
  6.8 0.0 copy-start.4
  6.8 0.8 %copy-done.4 = bf16[128,256]{1,0:T(8,128)(2,1)S(1)} copy-done((bf16[128,256]{1,0:T(8,128)(2,1)S(1)}, bf16[128,256]{1,0:T(8,128)(2,1)}, u32[]{:S(2)}) %copy-start.4) | copy-done | bytes 65560
  7.7 0.0 copy-start.5
  7.7 0.8 %copy-done.5 = bf16[128,256]{1,0:T(8,128)(2,1)S(1)} copy-done((bf16[128,256]{1,0:T(8,128)(2,1)S(1)}, bf16[128,256]{1,0:T(8,128)(2,1)}, u32[]{:S(2)}) %copy-start.5) | copy-done | bytes 65560
  8.5 0.0 copy-start.6
  8.5 0.8 %copy-done.6 = bf16[128,256]{1,0:T(8,128)(2,1)S(1)} copy-done((bf16[128,256]{1,0:T(8,128)(2,1)S(1)}, bf16[128,256]{1,0:T(8,128)(2,1)}, u32[]{:S(2)}) %copy-start.6) | copy-done | bytes 65560
  9.4 0.0 copy-start.7
  9.4 0.7 %copy-done.7 = s32[128]{0:T(128)S(1)} copy-done((s32[128]{0:T(128)S(1)}, s32[128]{0:T(128)}, u32[]{:S(2)}) %copy-start.7) | copy-done | bytes 536
  10.0 46.3 %shard_map.129 = (bf16[128,768]{1,0:T(8,128)(2,1)S(1)}, bf16[128,256]{1,0:T(8,128)(2,1)S(1)}, bf16[128,256]{1,0:T(8,128)(2,1)S(1)}, bf16[128,256]{1,0:T(8,128)(2,1)S(1)}) custom-call(bf16[128,192]{1,0:T(8,128)(2,1)S(1)} %copy.14.og_ref, s32[1,128]{1,0:T(1,128)S(1)} %bitcast.1, s32[8,1]{1,0:T(8,128)S(1)} %copy.15.counts_ref, ...), custom_call_target="tpu_custom_call" | custom-call | tf_op jit(solution)/shard_map/pallas_call | solution.py:298
  56.3 0.7 %copy.20 = bf16[128,768]{1,0:T(8,128)(2,1)} copy(bf16[128,768]{1,0:T(8,128)(2,1)S(1)} %get-tuple-element.8) | data formatting | bytes 393216
  57.0 0.6 %copy.21 = bf16[128,256]{1,0:T(8,128)(2,1)} copy(bf16[128,256]{1,0:T(8,128)(2,1)S(1)} %get-tuple-element.9) | data formatting | bytes 131072
  57.6 0.6 %copy.22 = bf16[128,256]{1,0:T(8,128)(2,1)} copy(bf16[128,256]{1,0:T(8,128)(2,1)S(1)} %get-tuple-element.10) | data formatting | bytes 131072
  58.2 0.6 %copy.23 = bf16[128,256]{1,0:T(8,128)(2,1)} copy(bf16[128,256]{1,0:T(8,128)(2,1)S(1)} %get-tuple-element.11) | data formatting | bytes 131072
Async XLA Ops:
  2.3 1.3 %copy-start = (bf16[1,768,768]{2,1,0:T(8,128)(2,1)S(1)}, bf16[1,768,768]{2,1,0:T(8,128)(2,1)}, u32[]{:S(2)}) copy-start(bf16[1,768,768]{2,1,0:T(8,128)(2,1)} %up_hbm.1) | copy-start | bytes 3538948
  3.5 1.3 %copy-start.1 = (bf16[1,768,768]{2,1,0:T(8,128)(2,1)S(1)}, bf16[1,768,768]{2,1,0:T(8,128)(2,1)}, u32[]{:S(2)}) copy-start(bf16[1,768,768]{2,1,0:T(8,128)(2,1)} %down_hbm.1) | copy-start | bytes 3538948
  4.8 1.0 %copy-start.2 = (bf16[320,768]{1,0:T(8,128)(2,1)S(1)}, bf16[320,768]{1,0:T(8,128)(2,1)}, u32[]{:S(2)}) copy-start(bf16[320,768]{1,0:T(8,128)(2,1)} %pre_hbm.1) | copy-start | bytes 1474564
  5.8 1.0 %copy-start.3 = (bf16[256,768]{1,0:T(8,128)(2,1)S(1)}, bf16[256,768]{1,0:T(8,128)(2,1)}, u32[]{:S(2)}) copy-start(bf16[256,768]{1,0:T(8,128)(2,1)} %wout_hbm.1) | copy-start | bytes 1179652
  6.8 0.8 %copy-start.4 = (bf16[128,256]{1,0:T(8,128)(2,1)S(1)}, bf16[128,256]{1,0:T(8,128)(2,1)}, u32[]{:S(2)}) copy-start(bf16[128,256]{1,0:T(8,128)(2,1)} %q_ref.1) | copy-start | bytes 196612
  7.7 0.8 %copy-start.5 = (bf16[128,256]{1,0:T(8,128)(2,1)S(1)}, bf16[128,256]{1,0:T(8,128)(2,1)}, u32[]{:S(2)}) copy-start(bf16[128,256]{1,0:T(8,128)(2,1)} %k_ref.1) | copy-start | bytes 196612
  8.5 0.8 %copy-start.6 = (bf16[128,256]{1,0:T(8,128)(2,1)S(1)}, bf16[128,256]{1,0:T(8,128)(2,1)}, u32[]{:S(2)}) copy-start(bf16[128,256]{1,0:T(8,128)(2,1)} %v_ref.1) | copy-start | bytes 196612
  9.4 0.7 %copy-start.7 = (s32[128]{0:T(128)S(1)}, s32[128]{0:T(128)}, u32[]{:S(2)}) copy-start(s32[128]{0:T(128)} %param.11) | copy-start | bytes 1540

commit v2 on v1

v2 whole, which is shorter than its diff:
```python
import functools
import math

import jax
import jax.numpy as jnp
from jax import lax
from jax.experimental import pallas as pl
from jax.experimental.pallas import tpu as pltpu
from jax.sharding import PartitionSpec as P

MESH = pl.DeviceIdType.MESH
F32 = jnp.float32
BF16 = jnp.bfloat16
ROWS = 16


def iota(shape, dim):
    return lax.broadcasted_iota(jnp.int32, shape, dim)


def nn(a, b):
    return jnp.dot(a, b, preferred_element_type=F32)


def nt(a, b):
    return lax.dot_general(a, b, (((1,), (1,)), ((), ())), preferred_element_type=F32)


def kernel(
    n, pad, scaling,
    og_hbm, expert_hbm, counts_hbm, up_hbm, down_hbm, pre_hbm, q_hbm, k_hbm, v_hbm, wout_hbm,
    gh, gq_out, gk_out, gv_out,
    expert_of, counts, up, down, pre, wout, q, k, v, mask, grad_t, xsend, x, hsum, hsend, hrecv,
    ysend, yrecv, rsend, ret, eg, eg_in, gh_all, ks_send, ks_recv, ks, qs_send, qs_recv, qs,
    load_sem, one_send, one_recv, disp_send, disp_recv, ax_send, ax_recv, as_send, as_recv,
    hs_send, hs_recv, hy_send, hy_recv, ret_send, ret_recv, st_send, st_recv,
):
    s = lax.axis_index("seq")
    h = lax.axis_index("head")
    c = lax.rem(h, 2)
    y = lax.div(h, 2)
    sib = (s, h + 1 - 2 * c)
    far = (s, lax.rem(h + 2, 4))
    m = n // 2
    width, tok = og_hbm.shape
    pair = 2 * width
    rows = m * pad
    depth = x.shape[2]
    piece = ks.shape[1]
    mine = pl.ds(pl.multiple_of(y * pair, 128), pair)
    other = pl.ds(pl.multiple_of((1 - y) * pair, 128), pair)
    parity = lax.rem(s + c, 2)
    own_rows = pl.ds(pl.multiple_of(c * width, ROWS), width)
    sib_rows = pl.ds(pl.multiple_of((1 - c) * width, ROWS), width)

    def send(src, dst, ssem, rsem, to):
        return pltpu.make_async_remote_copy(
            src_ref=src, dst_ref=dst, send_sem=ssem, recv_sem=rsem, device_id=to, device_id_type=MESH
        )

    barrier = pltpu.get_barrier_semaphore()
    peers = [lax.rem(s + d, n) for d in range(1, n)]
    for p in peers:
        pl.semaphore_signal(barrier, inc=1, device_id=(p, h), device_id_type=MESH)
    for to in (sib, far):
        pl.semaphore_signal(barrier, inc=1, device_id=to, device_id_type=MESH)
    loads = {}
    for i, (name, src, dst) in enumerate((
        ("expert", expert_hbm, expert_of), ("grad", og_hbm, grad_t.at[own_rows]),
        ("k", k_hbm, k), ("v", v_hbm, v), ("counts", counts_hbm, counts), ("pre", pre_hbm, pre),
        ("down", down_hbm.at[0], down), ("up", up_hbm.at[0], up), ("wout", wout_hbm, wout),
        ("q", q_hbm, q),
    )):
        loads[name] = pltpu.make_async_copy(src, dst, load_sem.at[i])
        loads[name].start()

    pl.semaphore_wait(barrier, n + 1)
    pending = []

    def start(copy):
        copy.start()
        pending.append(copy)
        return copy

    start(send(og_hbm, grad_t.at[own_rows], one_send.at[0], one_recv.at[0], sib))

    loads["expert"].wait()
    e_row = expert_of[...]
    eye = iota((tok, tok), 0) == iota((tok, tok), 1)
    e_col = jnp.sum(jnp.where(eye, e_row, 0), axis=1, keepdims=True)
    same = (e_col == e_row).astype(jnp.int32)
    below = iota((tok, tok), 0) < iota((tok, tok), 1)
    rank_row = jnp.sum(jnp.where(below, same, 0), axis=0, keepdims=True)
    live_row = lax.rem(e_row, 2) == parity
    slot_row = jnp.where(live_row, lax.div(e_row, 2) * pad + rank_row, -1)
    scatter = (iota((rows, tok), 0) == slot_row).astype(BF16)

    loads["grad"].wait()
    spot = grad_t.at[sib_rows]
    send(spot, spot, one_send.at[0], one_recv.at[0], sib).wait_recv()
    blocks = nt(scatter, grad_t[...]).astype(BF16)
    for i in range(m):
        xsend[i] = blocks[i * pad : (i + 1) * pad]
    turns = [*range(1, m), 0]
    order = [(j, lax.rem(s + c + 2 * j, n)) for j in turns]
    for j, p in order:
        copy = send(
            xsend.at[lax.div(p, 2)], x.at[c * m + lax.div(s, 2), :, mine],
            disp_send.at[j], disp_recv.at[lax.div(s, 2)], (p, h),
        )
        if j == 0:
            pl.when(c == 1)(copy.start)

            @pl.when(c == 0)
            def _():
                x[lax.div(s, 2), :, mine] = xsend[lax.div(s, 2)]
        else:
            start(copy)

    loads["counts"].wait()
    slot = iota((2 * rows, 1), 0)
    block = lax.div(slot, pad)
    source = 2 * lax.rem(block, m) + lax.rem(lax.div(block, m) + s, 2)
    before = iota((2 * rows, n), 1) < source
    packed = jnp.sum(jnp.where(before, counts[...], 0), axis=1, keepdims=True) + lax.rem(slot, pad)
    unpack = (iota((2 * rows, pre.shape[0]), 1) == packed).astype(BF16)
    loads["pre"].wait()
    mask[...] = nn(unpack, pre[...]).astype(BF16)

    for j, p in order:
        i = lax.div(p, 2)
        spot = x.at[c * m + i, :, mine]
        copy = send(spot, spot, disp_send.at[j], disp_recv.at[i], (p, h))
        if j == 0:
            pl.when(c == 1)(copy.wait_recv)
        else:
            copy.wait_recv()
        start(send(spot, spot, ax_send.at[j], ax_recv.at[j], far))
        start(send(spot, spot, as_send.at[j], as_recv.at[j], sib))

    loads["k"].wait()
    loads["v"].wait()
    ks_part = nn(k[...].T, v[...]).astype(BF16)
    for p in range(n):
        ks_send[p] = ks_part[p * piece : (p + 1) * piece]

    def state_scatter(at, source, dest):
        for d, p in enumerate(peers):
            start(send(source.at[p], dest.at[s], st_send.at[at, d], st_recv.at[at, s], (p, h)))
        dest[s] = source[s]

    def state_sum(at, dest, total):
        for p in peers:
            send(dest.at[p], dest.at[p], st_send.at[at, 0], st_recv.at[at, p], (p, h)).wait_recv()
        acc = dest[0].astype(F32)
        for p in range(1, n):
            acc = acc + dest[p].astype(F32)
        total[s] = acc.astype(BF16)
        for d, p in enumerate(peers):
            start(send(
                total.at[s], total.at[s], st_send.at[at + 1, d], st_recv.at[at + 1, s], (p, h)
            ))

    def state_wait(at, total):
        for p in peers:
            send(total.at[p], total.at[p], st_send.at[at, 0], st_recv.at[at, p], (p, h)).wait_recv()

    state_scatter(0, ks_send, ks_recv)

    for j, p in order:
        spot = x.at[c * m + lax.div(p, 2), :, other]
        send(spot, spot, ax_send.at[j], ax_recv.at[j], far).wait_recv()
        start(send(spot, spot, as_send.at[m + j], as_recv.at[m + j], sib))

    loads["down"].wait()
    loads["up"].wait()

    def expert(cls):
        xs = x[pl.ds(cls * m, m)].reshape(rows, depth)
        middle = nt(xs, down[...])
        live = mask[pl.ds(pl.multiple_of(cls * rows, ROWS), rows), :]
        mid = jnp.where(live > 0, middle, 0.0).astype(BF16)
        return nt(mid, up[...]).reshape(m, pad, depth)

    hsum[...] = expert(c)
    sib_order = [(j, lax.rem(s + 1 - c + 2 * j, n)) for j in turns]
    for j, p in sib_order:
        for first, half in ((0, mine), (m, other)):
            spot = x.at[(1 - c) * m + lax.div(p, 2), :, half]
            send(spot, spot, as_send.at[first + j], as_recv.at[first + j], sib).wait_recv()
    hsend[...] = expert(1 - c).astype(BF16)
    for j, p in sib_order:
        i = lax.div(p, 2)
        start(send(hsend.at[i], hrecv.at[i], hs_send.at[j], hs_recv.at[j], sib))
    state_sum(0, ks_recv, ks)
    for j, p in order:
        i = lax.div(p, 2)
        spot = hrecv.at[i]
        send(spot, spot, hs_send.at[j], hs_recv.at[j], sib).wait_recv()
        ysend[i] = (hsum[i, :, other] + hrecv[i, :, other].astype(F32)).astype(BF16)
        start(send(ysend.at[i], yrecv.at[i], hy_send.at[j], hy_recv.at[j], far))

    for j, p in order:
        i = lax.div(p, 2)
        own = hsum[i, :, mine] + hrecv[i, :, mine].astype(F32)
        spot = yrecv.at[i]
        send(spot, spot, hy_send.at[j], hy_recv.at[j], far).wait_recv()
        rsend[i] = (own + yrecv[i].astype(F32)).astype(BF16)
        copy = send(
            rsend.at[i], ret.at[lax.div(s, 2)], ret_send.at[j], ret_recv.at[lax.div(s, 2)], (p, h)
        )
        if j == 0:
            pl.when(c == 1)(copy.start)

            @pl.when(c == 0)
            def _():
                ret[lax.div(s, 2)] = rsend[lax.div(s, 2)]
        else:
            start(copy)
    above = iota((tok, tok), 1) < iota((tok, tok), 0)
    rank_col = jnp.sum(jnp.where(above, same, 0), axis=1, keepdims=True)
    live_col = lax.rem(e_col, 2) == parity
    slot_col = jnp.where(live_col, lax.div(e_col, 2) * pad + rank_col, -1)
    combine = (iota((tok, rows), 1) == slot_col).astype(BF16)
    own = grad_t[...].astype(F32).T
    loads["wout"].wait()
    loads["q"].wait()
    q_t = q[...].T
    for j, p in order:
        i = lax.div(p, 2)
        copy = send(ret.at[i], ret.at[i], ret_send.at[j], ret_recv.at[i], (p, h))
        if j == 0:
            pl.when(c == 1)(copy.wait_recv)
        else:
            copy.wait_recv()
    share = nn(combine, ret[...].reshape(rows, pair))
    eg[...] = share.astype(BF16)
    start(send(eg, eg_in, one_send.at[1], one_recv.at[1], sib))
    own = own + share
    send(eg, eg_in, one_send.at[1], one_recv.at[1], sib).wait_recv()
    half = (own + eg_in[...].astype(F32)).astype(BF16)
    gh_all[:, mine] = half
    spot = gh_all.at[:, mine]
    start(send(spot, spot, one_send.at[2], one_recv.at[2], far))
    head_part = nt(half, wout[:, mine])
    state_wait(1, ks)
    spot = gh_all.at[:, other]
    send(spot, spot, one_send.at[2], one_recv.at[2], far).wait_recv()
    head_grad = (head_part + nt(gh_all[:, other], wout[:, other])).astype(BF16)
    qs_part = nn(q_t, head_grad).astype(BF16)
    for p in range(n):
        qs_send[p] = qs_part[p * piece : (p + 1) * piece]
    state_scatter(2, qs_send, qs_recv)
    gh[...] = gh_all[...]
    dim = n * piece
    gq_out[...] = (scaling * nt(head_grad, ks[...].reshape(dim, dim))).astype(BF16)
    state_sum(2, qs_recv, qs)
    state_wait(3, qs)
    q_round = qs[...].reshape(dim, dim)
    gk_out[...] = (scaling * nt(v[...], q_round)).astype(BF16)
    gv_out[...] = (scaling * nn(k[...], q_round)).astype(BF16)

    for copy in pending:
        copy.wait_send()

    @pl.when(c == 1)
    def _():
        send(xsend.at[0], xsend.at[0], disp_send.at[0], disp_recv.at[0], sib).wait_send()
        send(rsend.at[0], rsend.at[0], ret_send.at[0], ret_recv.at[0], sib).wait_send()


def write_out(*refs):
    count = len(refs) // 2
    sem = refs[-1]
    copies = [pltpu.make_async_copy(refs[i], refs[count + i], sem.at[i]) for i in range(count)]
    for copy in copies:
        copy.start()
    for copy in copies:
        copy.wait()


def fused(out_grad, expert_of, counts, w_up, w_down, pre_act, queries, keys, values, w_out):
    n = lax.axis_size("seq")
    m = n // 2
    tok, width = out_grad.shape
    slots = pre_act.shape[0]
    cap = slots // n
    pad = -(-cap // ROWS) * ROWS
    rows = m * pad
    depth, hidden = w_up.shape[1:]
    dim = queries.shape[1]
    pair = 2 * width
    piece = dim // n
    scaling = 1.0 / math.sqrt(dim * tok * n)
    vmem = pl.BlockSpec(memory_space=pltpu.VMEM)
    hbm = pl.BlockSpec(memory_space=pltpu.HBM)
    dma = pltpu.SemaphoreType.DMA

    def buf(*shape, dtype=BF16):
        return pltpu.VMEM(shape, dtype)

    state = buf(n, piece, dim)
    out = jax.ShapeDtypeStruct((tok, dim), BF16)
    outs = (jax.ShapeDtypeStruct((tok, depth), BF16), out, out, out)
    results = pl.pallas_call(
        functools.partial(kernel, n, pad, scaling),
        out_shape=outs,
        in_specs=[hbm] * 10,
        out_specs=(vmem,) * 4,
        scratch_shapes=[
            buf(1, tok, dtype=jnp.int32), buf(1, n, dtype=jnp.int32),
            buf(depth, hidden), buf(hidden, depth), buf(slots, hidden), buf(dim, depth),
            buf(tok, dim), buf(tok, dim), buf(tok, dim), buf(2 * rows, hidden),
            buf(pair, tok), buf(m, pad, pair), buf(n, pad, depth),
            buf(m, pad, depth, dtype=F32), buf(m, pad, depth), buf(m, pad, depth),
            buf(m, pad, pair), buf(m, pad, pair), buf(m, pad, pair), buf(m, pad, pair),
            buf(tok, pair), buf(tok, pair), buf(tok, depth),
            state, state, state, state, state, state,
            dma((10,)), dma((3,)), dma((3,)), dma((m,)), dma((m,)), dma((m,)), dma((m,)),
            dma((n,)), dma((n,)), dma((m,)), dma((m,)), dma((m,)), dma((m,)), dma((m,)), dma((m,)),
            dma((4, n)), dma((4, n)),
        ],
        compiler_params=pltpu.CompilerParams(
            collective_id=0, has_side_effects=True, vmem_limit_bytes=48 * 1024 * 1024
        ),
    )(*(pltpu.with_memory_space_constraint(operand, pltpu.HBM) for operand in (
        out_grad.T, expert_of.reshape(1, tok), counts.T, w_up, w_down, pre_act,
        queries, keys, values, w_out,
    )))
    return pl.pallas_call(
        write_out,
        out_shape=outs,
        in_specs=[vmem] * 4,
        out_specs=(hbm,) * 4,
        scratch_shapes=[dma((4,))],
    )(*results)


def step(*arrays):
    n, heads = lax.axis_size("seq"), lax.axis_size("head")
    width, dim = arrays[0].shape[1], arrays[6].shape[1]
    fits = heads == 4 and n % 2 == 0 and dim % (n * ROWS) == 0 and 2 * width % 128 == 0
    return (fused if fits else shards)(*arrays)


def shards(out_grad, expert_of, counts, w_up, w_down, pre_act, queries, keys, values, w_out):
    experts = lax.axis_size("seq")
    tok_rows = out_grad.shape[0]
    slot_count = pre_act.shape[0]
    capacity = slot_count // experts
    head_dim = queries.shape[1]
    scaling = 1.0 / math.sqrt(head_dim * tok_rows * experts)
    full_rows = lax.all_gather(out_grad, "head", axis=1, tiled=True)
    expert_ids = jnp.arange(experts, dtype=jnp.int32)
    onehot = (expert_of[:, None] == expert_ids[None, :]).astype(jnp.int32)
    token_rank = jnp.sum((jnp.cumsum(onehot, axis=0) - 1) * onehot, axis=1)
    slot_of = expert_of * capacity + token_rank
    token_of_slot = (
        jnp.full((experts * capacity,), tok_rows, jnp.int32)
        .at[slot_of]
        .set(jnp.arange(tok_rows, dtype=jnp.int32))
    )
    arrived = counts[:, 0]
    offsets = jnp.cumsum(arrived) - arrived
    arrived_total = jnp.sum(arrived)
    packed_ids = jnp.arange(slot_count, dtype=jnp.int32)
    source = jnp.sum((offsets[None, :] <= packed_ids[:, None]).astype(jnp.int32), axis=1) - 1
    within = packed_ids - offsets[source]
    packed_live = packed_ids < arrived_total
    flat_pos = jnp.where(packed_live, source * capacity + within, experts * capacity)
    down_local = w_down[0]
    up_local = w_up[0]
    padded = jnp.concatenate(
        [full_rows, jnp.zeros((1, full_rows.shape[1]), full_rows.dtype)], axis=0
    )
    received = lax.all_to_all(
        padded[token_of_slot].reshape(experts, capacity, full_rows.shape[1]),
        "seq",
        split_axis=0,
        concat_axis=0,
        tiled=True,
    )
    flat_rows = received.reshape(experts * capacity, received.shape[2])
    padded = jnp.concatenate(
        [flat_rows, jnp.zeros((1, flat_rows.shape[1]), flat_rows.dtype)], axis=0
    )
    middle = jnp.dot(padded[flat_pos], down_local.T, preferred_element_type=jnp.float32)
    mid_grad = jnp.where(pre_act > 0, middle, jnp.zeros_like(middle)).astype(jnp.bfloat16)
    hidden_part = jnp.dot(mid_grad, up_local.T, preferred_element_type=jnp.float32)
    slot_ids = jnp.arange(experts * capacity, dtype=jnp.int32)
    slot_source = slot_ids // capacity
    slot_rank = slot_ids % capacity
    slot_live = slot_rank < arrived[slot_source]
    slot_pos = jnp.where(slot_live, offsets[slot_source] + slot_rank, slot_count)
    share_packed = lax.psum_scatter(
        hidden_part.astype(jnp.bfloat16), "head", scatter_dimension=1, tiled=True
    )
    share_width = share_packed.shape[1]
    padded_grad = jnp.concatenate(
        [share_packed, jnp.zeros((1, share_packed.shape[1]), jnp.bfloat16)], axis=0
    )
    returned = lax.all_to_all(
        padded_grad[slot_pos].reshape(experts, capacity, share_packed.shape[1]),
        "seq",
        split_axis=0,
        concat_axis=0,
        tiled=True,
    )
    share_grad = returned.reshape(experts * capacity, share_width)[slot_of]
    expert_grad = lax.all_gather(share_grad, "head", axis=1, tiled=True)
    grad_hidden = (full_rows.astype(jnp.float32) + expert_grad.astype(jnp.float32)).astype(
        jnp.bfloat16
    )
    head_grad = jnp.dot(grad_hidden, w_out.T, preferred_element_type=jnp.float32).astype(
        jnp.bfloat16
    )
    query_part = jnp.dot(queries.T, head_grad, preferred_element_type=jnp.float32)
    key_state, query_state = lax.psum(
        (jnp.dot(keys.T, values, preferred_element_type=jnp.float32), query_part), "seq"
    )
    key_round = key_state.astype(jnp.bfloat16)
    query_round = query_state.astype(jnp.bfloat16)
    grad_queries = (
        scaling * jnp.dot(head_grad, key_round.T, preferred_element_type=jnp.float32)
    ).astype(jnp.bfloat16)
    grad_keys = (
        scaling * jnp.dot(values, query_round.T, preferred_element_type=jnp.float32)
    ).astype(jnp.bfloat16)
    grad_values = (scaling * jnp.dot(keys, query_round, preferred_element_type=jnp.float32)).astype(
        jnp.bfloat16
    )
    return (grad_hidden, grad_queries, grad_keys, grad_values)


def solution(mesh):
    return jax.shard_map(
        step,
        mesh=mesh,
        in_specs=(
            P("seq", "head"),
            P("seq"),
            P(None, "seq"),
            P("seq", None, "head"),
            P("seq", "head", None),
            P("seq", "head"),
            P("seq", "head"),
            P("seq", "head"),
            P("seq", "head"),
            P("head", None),
        ),
        out_specs=(P("seq", None), P("seq", "head"), P("seq", "head"), P("seq", "head")),
        check_vma=False,
    )
```

time: 59.4 us -> 49.7 us (0.84)
  local copies, waits for them, and re-layouts: 11.9 us -> 2.52 us
    unnamed x22 -> x8, local copies, waits for them, and re-layouts: 11.9 us -> 2.52 us
    pallas_call x1 -> x2, Pallas kernels: 46.3 us -> 46.4 us  [the longest x1 44.6 us: fused(): pl.pallas_call(functools.partial(kernel, n, pad, scaling), out_shape=outs...]
where the time goes in v2:
time: 49.7 us; the launch traced here: 49.5 us
  Pallas kernels  46.4 us (93%)
  local copies, waits for them, and re-layouts  2.52 us (5%)
  between operations  0.65 us (1%)
    pallas_call x1, Pallas kernels, fused(): pl.pallas_call(functools.partial(kernel, n, pad, scaling), out_shape=outs...  44.6 us
    unnamed x8, local copies, waits for them, and re-layouts  2.52 us
    pallas_call x1, Pallas kernels, fused(): pl.pallas_call(write_out, out_shape=outs, in_specs=[vmem] * 4, out_specs=...  1.77 us

profile of v2, /device:TPU:0, one launch (start us, length us, event | category | flops | bytes accessed | tf_op | source)
XLA Modules:
  0.0 49.5 jit_solution(10120711277295748640)
XLA Ops:
  0.6 44.6 %shard_map.129 = (bf16[128,768]{1,0:T(8,128)(2,1)S(1)}, bf16[128,256]{1,0:T(8,128)(2,1)S(1)}, bf16[128,256]{1,0:T(8,128)(2,1)S(1)}, bf16[128,256]{1,0:T(8,128)(2,1)S(1)}) custom-call(bf16[192,128]{1,0:T(8,128)(2,1)} %bitcast.3, s32[1,128]{1,0:T(1,128)} %bitcast.4, s32[1,8]{1,0:T(1,128)} %bitcast.5, bf16[1,768,768]{2,1,0:T(8,128)(2,1)} %up_hbm.1, ...), custom_call_target="tpu_custom_call" | custom-call | tf_op jit(solution)/shard_map/pallas_call | solution.py:305
  45.2 0.0 copy-start
  45.2 0.7 %copy-done = bf16[128,768]{1,0:T(8,128)(2,1)} copy-done((bf16[128,768]{1,0:T(8,128)(2,1)}, bf16[128,768]{1,0:T(8,128)(2,1)S(1)}, u32[]{:S(2)}) %copy-start) | copy-done | bytes 196632
  45.9 0.0 copy-start.1
  45.9 0.6 %copy-done.1 = bf16[128,256]{1,0:T(8,128)(2,1)} copy-done((bf16[128,256]{1,0:T(8,128)(2,1)}, bf16[128,256]{1,0:T(8,128)(2,1)S(1)}, u32[]{:S(2)}) %copy-start.1) | copy-done | bytes 65560
  46.5 0.0 copy-start.2
  46.5 0.6 %copy-done.2 = bf16[128,256]{1,0:T(8,128)(2,1)} copy-done((bf16[128,256]{1,0:T(8,128)(2,1)}, bf16[128,256]{1,0:T(8,128)(2,1)S(1)}, u32[]{:S(2)}) %copy-start.2) | copy-done | bytes 65560
  47.1 0.0 copy-start.3
  47.1 0.6 %copy-done.3 = bf16[128,256]{1,0:T(8,128)(2,1)} copy-done((bf16[128,256]{1,0:T(8,128)(2,1)}, bf16[128,256]{1,0:T(8,128)(2,1)S(1)}, u32[]{:S(2)}) %copy-start.3) | copy-done | bytes 65560
  47.8 1.8 %shard_map.130 = (bf16[128,768]{1,0:T(8,128)(2,1)}, bf16[128,256]{1,0:T(8,128)(2,1)}, bf16[128,256]{1,0:T(8,128)(2,1)}, bf16[128,256]{1,0:T(8,128)(2,1)}) custom-call(bf16[128,768]{1,0:T(8,128)(2,1)} %copy-done, bf16[128,256]{1,0:T(8,128)(2,1)} %copy-done.1, bf16[128,256]{1,0:T(8,128)(2,1)} %copy-done.2, bf16[128,256]{1,0:T(8,128)(2,1)} %copy-done.3), custom_call_target="tpu_custom_call" | custom-call | tf_op jit(solution)/shard_map/pallas_call | solution.py:330
Async XLA Ops:
  45.2 0.7 %copy-start = (bf16[128,768]{1,0:T(8,128)(2,1)}, bf16[128,768]{1,0:T(8,128)(2,1)S(1)}, u32[]{:S(2)}) copy-start(bf16[128,768]{1,0:T(8,128)(2,1)S(1)} %get-tuple-element.8.refs_0_) | copy-start | bytes 589828
  45.9 0.6 %copy-start.1 = (bf16[128,256]{1,0:T(8,128)(2,1)}, bf16[128,256]{1,0:T(8,128)(2,1)S(1)}, u32[]{:S(2)}) copy-start(bf16[128,256]{1,0:T(8,128)(2,1)S(1)} %get-tuple-element.9.refs_1_) | copy-start | bytes 196612
  46.5 0.6 %copy-start.2 = (bf16[128,256]{1,0:T(8,128)(2,1)}, bf16[128,256]{1,0:T(8,128)(2,1)S(1)}, u32[]{:S(2)}) copy-start(bf16[128,256]{1,0:T(8,128)(2,1)S(1)} %get-tuple-element.10.refs_2_) | copy-start | bytes 196612
  47.1 0.6 %copy-start.3 = (bf16[128,256]{1,0:T(8,128)(2,1)}, bf16[128,256]{1,0:T(8,128)(2,1)S(1)}, u32[]{:S(2)}) copy-start(bf16[128,256]{1,0:T(8,128)(2,1)S(1)} %get-tuple-element.11.refs_3_) | copy-start | bytes 196612

commit v3 on v2

--- a/solution.py
+++ b/solution.py
@@ -12,6 +12,7 @@
 F32 = jnp.float32
 BF16 = jnp.bfloat16
 ROWS = 16
+VMEM_BYTES = 63 * 1024 * 1024
 
 
 def iota(shape, dim):
@@ -29,11 +30,12 @@
 def kernel(
     n, pad, scaling,
     og_hbm, expert_hbm, counts_hbm, up_hbm, down_hbm, pre_hbm, q_hbm, k_hbm, v_hbm, wout_hbm,
-    gh, gq_out, gk_out, gv_out,
-    expert_of, counts, up, down, pre, wout, q, k, v, mask, grad_t, xsend, x, hsum, hsend, hrecv,
-    ysend, yrecv, rsend, ret, eg, eg_in, gh_all, ks_send, ks_recv, ks, qs_send, qs_recv, qs,
-    load_sem, one_send, one_recv, disp_send, disp_recv, ax_send, ax_recv, as_send, as_recv,
-    hs_send, hs_recv, hy_send, hy_recv, ret_send, ret_recv, st_send, st_recv,
+    gh_out, gq_out, gk_out, gv_out,
+    expert_of, counts, up, down, pre, wout, q, k, v, mask, grad_t, xsend, x, hsum,
+    ysend, yrecv, rsend, ret, eg, eg_in, gh, ks_send, ks_recv, ks, qs_send, qs_recv, qs,
+    gq, gk, gv,
+    load_sem, one_send, one_recv, disp_send, disp_recv, ax_send, ax_recv,
+    hy_send, hy_recv, ret_send, ret_recv, st_send, st_recv, out_sem,
 ):
     s = lax.axis_index("seq")
     h = lax.axis_index("head")
@@ -67,8 +69,9 @@
     loads = {}
     for i, (name, src, dst) in enumerate((
         ("expert", expert_hbm, expert_of), ("grad", og_hbm, grad_t.at[own_rows]),
-        ("k", k_hbm, k), ("v", v_hbm, v), ("counts", counts_hbm, counts), ("pre", pre_hbm, pre),
-        ("down", down_hbm.at[0], down), ("up", up_hbm.at[0], up), ("wout", wout_hbm, wout),
+        ("k", k_hbm, k), ("v", v_hbm, v), ("counts", counts_hbm, counts),
+        ("pre", pre_hbm, pre.at[0]), ("down", down_hbm.at[0], down.at[0]),
+        ("up", up_hbm.at[0], up.at[0]), ("wout", wout_hbm, wout),
         ("q", q_hbm, q),
     )):
         loads[name] = pltpu.make_async_copy(src, dst, load_sem.at[i])
@@ -83,6 +86,12 @@
         return copy
 
     start(send(og_hbm, grad_t.at[own_rows], one_send.at[0], one_recv.at[0], sib))
+    swaps = [
+        start(send(src, dst, one_send.at[3 + i], one_recv.at[3 + i], sib))
+        for i, (src, dst) in enumerate((
+            (pre_hbm, pre.at[1]), (down_hbm.at[0], down.at[1]), (up_hbm.at[0], up.at[1])
+        ))
+    ]
 
     loads["expert"].wait()
     e_row = expert_of[...]
@@ -105,7 +114,7 @@
     order = [(j, lax.rem(s + c + 2 * j, n)) for j in turns]
     for j, p in order:
         copy = send(
-            xsend.at[lax.div(p, 2)], x.at[c * m + lax.div(s, 2), :, mine],
+            xsend.at[lax.div(p, 2)], x.at[lax.div(s, 2), :, mine],
             disp_send.at[j], disp_recv.at[lax.div(s, 2)], (p, h),
         )
         if j == 0:
@@ -118,25 +127,23 @@
             start(copy)
 
     loads["counts"].wait()
-    slot = iota((2 * rows, 1), 0)
-    block = lax.div(slot, pad)
-    source = 2 * lax.rem(block, m) + lax.rem(lax.div(block, m) + s, 2)
-    before = iota((2 * rows, n), 1) < source
+    slot = iota((rows, 1), 0)
+    source = 2 * lax.div(slot, pad) + parity
+    before = iota((rows, n), 1) < source
     packed = jnp.sum(jnp.where(before, counts[...], 0), axis=1, keepdims=True) + lax.rem(slot, pad)
-    unpack = (iota((2 * rows, pre.shape[0]), 1) == packed).astype(BF16)
+    unpack = (iota((rows, pre.shape[1]), 1) == packed).astype(BF16)
     loads["pre"].wait()
-    mask[...] = nn(unpack, pre[...]).astype(BF16)
+    mask[0] = nn(unpack, pre[0]).astype(BF16)
 
     for j, p in order:
         i = lax.div(p, 2)
-        spot = x.at[c * m + i, :, mine]
+        spot = x.at[i, :, mine]
         copy = send(spot, spot, disp_send.at[j], disp_recv.at[i], (p, h))
         if j == 0:
             pl.when(c == 1)(copy.wait_recv)
         else:
             copy.wait_recv()
         start(send(spot, spot, ax_send.at[j], ax_recv.at[j], far))
-        start(send(spot, spot, as_send.at[j], as_recv.at[j], sib))
 
     loads["k"].wait()
     loads["v"].wait()
@@ -167,45 +174,36 @@
 
     state_scatter(0, ks_send, ks_recv)
 
-    for j, p in order:
-        spot = x.at[c * m + lax.div(p, 2), :, other]
+    swaps[0].wait_recv()
+    mask[1] = nn(unpack, pre[1]).astype(BF16)
+    loads["down"].wait()
+    swaps[1].wait_recv()
+    ready = x[:, :, mine].reshape(rows, pair)
+    middle = [nt(ready, down[u, :, mine]) for u in range(2)]
+    loads["up"].wait()
+    swaps[2].wait_recv()
+    for j, p in order:
+        spot = x.at[lax.div(p, 2), :, other]
         send(spot, spot, ax_send.at[j], ax_recv.at[j], far).wait_recv()
-        start(send(spot, spot, as_send.at[m + j], as_recv.at[m + j], sib))
-
-    loads["down"].wait()
-    loads["up"].wait()
-
-    def expert(cls):
-        xs = x[pl.ds(cls * m, m)].reshape(rows, depth)
-        middle = nt(xs, down[...])
-        live = mask[pl.ds(pl.multiple_of(cls * rows, ROWS), rows), :]
-        mid = jnp.where(live > 0, middle, 0.0).astype(BF16)
-        return nt(mid, up[...]).reshape(m, pad, depth)
-
-    hsum[...] = expert(c)
-    sib_order = [(j, lax.rem(s + 1 - c + 2 * j, n)) for j in turns]
-    for j, p in sib_order:
-        for first, half in ((0, mine), (m, other)):
-            spot = x.at[(1 - c) * m + lax.div(p, 2), :, half]
-            send(spot, spot, as_send.at[first + j], as_recv.at[first + j], sib).wait_recv()
-    hsend[...] = expert(1 - c).astype(BF16)
-    for j, p in sib_order:
+    ready = x[:, :, other].reshape(rows, pair)
+    mid = [
+        jnp.where(mask[u] > 0, middle[u] + nt(ready, down[u, :, other]), 0.0).astype(BF16)
+        for u in range(2)
+    ]
+    ysend[...] = (nt(mid[0], up[0, other, :]) + nt(mid[1], up[1, other, :])).astype(BF16).reshape(
+        m, pad, pair
+    )
+    for j, p in order:
         i = lax.div(p, 2)
-        start(send(hsend.at[i], hrecv.at[i], hs_send.at[j], hs_recv.at[j], sib))
+        start(send(ysend.at[i], yrecv.at[i], hy_send.at[j], hy_recv.at[j], far))
+    hsum[...] = (nt(mid[0], up[0, mine, :]) + nt(mid[1], up[1, mine, :])).reshape(m, pad, pair)
     state_sum(0, ks_recv, ks)
+
     for j, p in order:
         i = lax.div(p, 2)
-        spot = hrecv.at[i]
-        send(spot, spot, hs_send.at[j], hs_recv.at[j], sib).wait_recv()
-        ysend[i] = (hsum[i, :, other] + hrecv[i, :, other].astype(F32)).astype(BF16)
-        start(send(ysend.at[i], yrecv.at[i], hy_send.at[j], hy_recv.at[j], far))
-
-    for j, p in order:
-        i = lax.div(p, 2)
-        own = hsum[i, :, mine] + hrecv[i, :, mine].astype(F32)
         spot = yrecv.at[i]
         send(spot, spot, hy_send.at[j], hy_recv.at[j], far).wait_recv()
-        rsend[i] = (own + yrecv[i].astype(F32)).astype(BF16)
+        rsend[i] = (hsum[i] + yrecv[i].astype(F32)).astype(BF16)
         copy = send(
             rsend.at[i], ret.at[lax.div(s, 2)], ret_send.at[j], ret_recv.at[lax.div(s, 2)], (p, h)
         )
@@ -239,29 +237,40 @@
     own = own + share
     send(eg, eg_in, one_send.at[1], one_recv.at[1], sib).wait_recv()
     half = (own + eg_in[...].astype(F32)).astype(BF16)
-    gh_all[:, mine] = half
-    spot = gh_all.at[:, mine]
+    gh[:, mine] = half
+    spot = gh.at[:, mine]
     start(send(spot, spot, one_send.at[2], one_recv.at[2], far))
     head_part = nt(half, wout[:, mine])
     state_wait(1, ks)
-    spot = gh_all.at[:, other]
+    spot = gh.at[:, other]
     send(spot, spot, one_send.at[2], one_recv.at[2], far).wait_recv()
-    head_grad = (head_part + nt(gh_all[:, other], wout[:, other])).astype(BF16)
+    head_grad = (head_part + nt(gh[:, other], wout[:, other])).astype(BF16)
     qs_part = nn(q_t, head_grad).astype(BF16)
     for p in range(n):
         qs_send[p] = qs_part[p * piece : (p + 1) * piece]
     state_scatter(2, qs_send, qs_recv)
-    gh[...] = gh_all[...]
+    writes = []
+
+    def write(src, dst):
+        writes.append(pltpu.make_async_copy(src, dst, out_sem.at[len(writes)]))
+        writes[-1].start()
+
+    write(gh, gh_out)
     dim = n * piece
-    gq_out[...] = (scaling * nt(head_grad, ks[...].reshape(dim, dim))).astype(BF16)
+    gq[...] = (scaling * nt(head_grad, ks[...].reshape(dim, dim))).astype(BF16)
+    write(gq, gq_out)
     state_sum(2, qs_recv, qs)
     state_wait(3, qs)
     q_round = qs[...].reshape(dim, dim)
-    gk_out[...] = (scaling * nt(v[...], q_round)).astype(BF16)
-    gv_out[...] = (scaling * nn(k[...], q_round)).astype(BF16)
+    gk[...] = (scaling * nt(v[...], q_round)).astype(BF16)
+    write(gk, gk_out)
+    gv[...] = (scaling * nn(k[...], q_round)).astype(BF16)
+    write(gv, gv_out)
 
     for copy in pending:
         copy.wait_send()
+    for copy in writes:
+        copy.wait()
 
     @pl.when(c == 1)
     def _():
@@ -292,8 +301,8 @@
     pair = 2 * width
     piece = dim // n
     scaling = 1.0 / math.sqrt(dim * tok * n)
-    vmem = pl.BlockSpec(memory_space=pltpu.VMEM)
     hbm = pl.BlockSpec(memory_space=pltpu.HBM)
+    anywhere = pl.BlockSpec(memory_space=pl.ANY)
     dma = pltpu.SemaphoreType.DMA
 
     def buf(*shape, dtype=BF16):
@@ -306,22 +315,21 @@
         functools.partial(kernel, n, pad, scaling),
         out_shape=outs,
         in_specs=[hbm] * 10,
-        out_specs=(vmem,) * 4,
+        out_specs=(anywhere,) * 4,
         scratch_shapes=[
             buf(1, tok, dtype=jnp.int32), buf(1, n, dtype=jnp.int32),
-            buf(depth, hidden), buf(hidden, depth), buf(slots, hidden), buf(dim, depth),
-            buf(tok, dim), buf(tok, dim), buf(tok, dim), buf(2 * rows, hidden),
-            buf(pair, tok), buf(m, pad, pair), buf(n, pad, depth),
-            buf(m, pad, depth, dtype=F32), buf(m, pad, depth), buf(m, pad, depth),
+            buf(2, depth, hidden), buf(2, hidden, depth), buf(2, slots, hidden), buf(dim, depth),
+            buf(tok, dim), buf(tok, dim), buf(tok, dim), buf(2, rows, hidden),
+            buf(pair, tok), buf(m, pad, pair), buf(m, pad, depth), buf(m, pad, pair, dtype=F32),
             buf(m, pad, pair), buf(m, pad, pair), buf(m, pad, pair), buf(m, pad, pair),
             buf(tok, pair), buf(tok, pair), buf(tok, depth),
             state, state, state, state, state, state,
-            dma((10,)), dma((3,)), dma((3,)), dma((m,)), dma((m,)), dma((m,)), dma((m,)),
-            dma((n,)), dma((n,)), dma((m,)), dma((m,)), dma((m,)), dma((m,)), dma((m,)), dma((m,)),
-            dma((4, n)), dma((4, n)),
+            buf(tok, dim), buf(tok, dim), buf(tok, dim),
+            dma((10,)), dma((6,)), dma((6,)), dma((m,)), dma((m,)), dma((m,)), dma((m,)),
+            dma((m,)), dma((m,)), dma((m,)), dma((m,)), dma((4, n)), dma((4, n)), dma((4,)),
         ],
         compiler_params=pltpu.CompilerParams(
-            collective_id=0, has_side_effects=True, vmem_limit_bytes=48 * 1024 * 1024
+            collective_id=0, has_side_effects=True, vmem_limit_bytes=VMEM_BYTES
         ),
     )(*(pltpu.with_memory_space_constraint(operand, pltpu.HBM) for operand in (
         out_grad.T, expert_of.reshape(1, tok), counts.T, w_up, w_down, pre_act,
@@ -330,9 +338,10 @@
     return pl.pallas_call(
         write_out,
         out_shape=outs,
-        in_specs=[vmem] * 4,
+        in_specs=[anywhere] * 4,
         out_specs=(hbm,) * 4,
         scratch_shapes=[dma((4,))],
+        compiler_params=pltpu.CompilerParams(vmem_limit_bytes=VMEM_BYTES),
     )(*results)
 
 

time: 49.7 us -> 57.2 us (1.15)
  Pallas kernels: 46.4 us -> 56.4 us
  local copies, waits for them, and re-layouts: 2.52 us -> 0 us
    pallas_call x1, Pallas kernels: 1.77 us -> 13.1 us  [fused(): pl.pallas_call(write_out, out_shape=outs, in_specs=[anywhere] * 4, out_sp...]
    unnamed x8 -> x0, local copies, waits for them, and re-layouts: 2.52 us -> none
    pallas_call x1, Pallas kernels: 44.6 us -> 43.3 us  [fused(): pl.pallas_call(functools.partial(kernel, n, pad, scaling), out_shape=outs...]
where the time goes in v3:
time: 57.2 us; the launch traced here: 57 us
  Pallas kernels  56.4 us (99%)
  between operations  0.64 us (1%)
    pallas_call x1, Pallas kernels, fused(): pl.pallas_call(functools.partial(kernel, n, pad, scaling), out_shape=outs...  43.3 us
    pallas_call x1, Pallas kernels, fused(): pl.pallas_call(write_out, out_shape=outs, in_specs=[anywhere] * 4, out_sp...  13.1 us

profile of v3, /device:TPU:0, one launch (start us, length us, event | category | flops | bytes accessed | tf_op | source)
XLA Modules:
  0.0 57.0 jit_solution(10023559053173158947)
XLA Ops:
  0.6 43.3 %shard_map.129 = (bf16[128,768]{1,0:T(8,128)(2,1)}, bf16[128,256]{1,0:T(8,128)(2,1)}, bf16[128,256]{1,0:T(8,128)(2,1)}, bf16[128,256]{1,0:T(8,128)(2,1)}) custom-call(bf16[192,128]{1,0:T(8,128)(2,1)} %bitcast.3, s32[1,128]{1,0:T(1,128)} %bitcast.4, s32[1,8]{1,0:T(1,128)} %bitcast.5, bf16[1,768,768]{2,1,0:T(8,128)(2,1)} %up_hbm.1, ...), custom_call_target="tpu_custom_call" | custom-call | tf_op jit(solution)/shard_map/pallas_call | solution.py:314
  44.0 13.1 %shard_map.130 = (bf16[128,768]{1,0:T(8,128)(2,1)}, bf16[128,256]{1,0:T(8,128)(2,1)}, bf16[128,256]{1,0:T(8,128)(2,1)}, bf16[128,256]{1,0:T(8,128)(2,1)}) custom-call(bf16[128,768]{1,0:T(8,128)(2,1)} %get-tuple-element.8.refs_0_, bf16[128,256]{1,0:T(8,128)(2,1)} %get-tuple-element.9.refs_1_, bf16[128,256]{1,0:T(8,128)(2,1)} %get-tuple-element.10.refs_2_, ...), custom_call_target="tpu_custom_call" | custom-call | tf_op jit(solution)/shard_map/pallas_call | solution.py:338

commit v4 on v3

--- a/solution.py
+++ b/solution.py
@@ -85,13 +85,13 @@
         pending.append(copy)
         return copy
 
-    start(send(og_hbm, grad_t.at[own_rows], one_send.at[0], one_recv.at[0], sib))
-    swaps = [
-        start(send(src, dst, one_send.at[3 + i], one_recv.at[3 + i], sib))
-        for i, (src, dst) in enumerate((
-            (pre_hbm, pre.at[1]), (down_hbm.at[0], down.at[1]), (up_hbm.at[0], up.at[1])
-        ))
-    ]
+    loads["grad"].wait()
+    spot = grad_t.at[own_rows]
+    start(send(spot, spot, one_send.at[0], one_recv.at[0], sib))
+    swaps = []
+    for i, (name, both) in enumerate((("pre", pre), ("down", down), ("up", up))):
+        loads[name].wait()
+        swaps.append(start(send(both.at[0], both.at[1], one_send.at[3 + i], one_recv.at[3 + i], sib)))
 
     loads["expert"].wait()
     e_row = expert_of[...]
@@ -104,7 +104,6 @@
     slot_row = jnp.where(live_row, lax.div(e_row, 2) * pad + rank_row, -1)
     scatter = (iota((rows, tok), 0) == slot_row).astype(BF16)
 
-    loads["grad"].wait()
     spot = grad_t.at[sib_rows]
     send(spot, spot, one_send.at[0], one_recv.at[0], sib).wait_recv()
     blocks = nt(scatter, grad_t[...]).astype(BF16)
@@ -132,7 +131,6 @@
     before = iota((rows, n), 1) < source
     packed = jnp.sum(jnp.where(before, counts[...], 0), axis=1, keepdims=True) + lax.rem(slot, pad)
     unpack = (iota((rows, pre.shape[1]), 1) == packed).astype(BF16)
-    loads["pre"].wait()
     mask[0] = nn(unpack, pre[0]).astype(BF16)
 
     for j, p in order:
@@ -176,11 +174,9 @@
 
     swaps[0].wait_recv()
     mask[1] = nn(unpack, pre[1]).astype(BF16)
-    loads["down"].wait()
     swaps[1].wait_recv()
     ready = x[:, :, mine].reshape(rows, pair)
     middle = [nt(ready, down[u, :, mine]) for u in range(2)]
-    loads["up"].wait()
     swaps[2].wait_recv()
     for j, p in order:
         spot = x.at[lax.div(p, 2), :, other]
@@ -279,12 +275,15 @@
 
 
 def write_out(*refs):
-    count = len(refs) // 2
-    sem = refs[-1]
-    copies = [pltpu.make_async_copy(refs[i], refs[count + i], sem.at[i]) for i in range(count)]
-    for copy in copies:
+    sources, dests, rooms, (come, go) = refs[:4], refs[4:8], refs[8:12], refs[12:]
+    ins = [pltpu.make_async_copy(a, b, come.at[i]) for i, (a, b) in enumerate(zip(sources, rooms))]
+    outs = [pltpu.make_async_copy(a, b, go.at[i]) for i, (a, b) in enumerate(zip(rooms, dests))]
+    for copy in ins:
         copy.start()
-    for copy in copies:
+    for first, second in zip(ins, outs):
+        first.wait()
+        second.start()
+    for copy in outs:
         copy.wait()
 
 
@@ -340,7 +339,7 @@
         out_shape=outs,
         in_specs=[anywhere] * 4,
         out_specs=(hbm,) * 4,
-        scratch_shapes=[dma((4,))],
+        scratch_shapes=[*(buf(*a.shape) for a in outs), dma((4,)), dma((4,))],
         compiler_params=pltpu.CompilerParams(vmem_limit_bytes=VMEM_BYTES),
     )(*results)
 

time: 57.2 us -> 45.6 us (0.80)
  Pallas kernels: 56.4 us -> 44.8 us
    pallas_call x1, Pallas kernels: 13.1 us -> 1.73 us  [fused(): pl.pallas_call(write_out, out_shape=outs, in_specs=[anywhere] * 4, out_sp...]
where the time goes in v4:
time: 45.6 us; the launch traced here: 45.4 us
  Pallas kernels  44.8 us (98%)
  between operations  0.64 us (1%)
    pallas_call x1, Pallas kernels, fused(): pl.pallas_call(functools.partial(kernel, n, pad, scaling), out_shape=outs...  43 us
    pallas_call x1, Pallas kernels, fused(): pl.pallas_call(write_out, out_shape=outs, in_specs=[anywhere] * 4, out_sp...  1.73 us

profile of v4, /device:TPU:0, one launch (start us, length us, event | category | flops | bytes accessed | tf_op | source)
XLA Modules:
  0.0 45.4 jit_solution(2506889250636948469)
XLA Ops:
  0.6 43.0 %shard_map.129 = (bf16[128,768]{1,0:T(8,128)(2,1)}, bf16[128,256]{1,0:T(8,128)(2,1)}, bf16[128,256]{1,0:T(8,128)(2,1)}, bf16[128,256]{1,0:T(8,128)(2,1)}) custom-call(bf16[192,128]{1,0:T(8,128)(2,1)} %bitcast.3, s32[1,128]{1,0:T(1,128)} %bitcast.4, s32[1,8]{1,0:T(1,128)} %bitcast.5, bf16[1,768,768]{2,1,0:T(8,128)(2,1)} %up_hbm.1, ...), custom_call_target="tpu_custom_call" | custom-call | tf_op jit(solution)/shard_map/pallas_call | solution.py:313
  43.7 1.7 %shard_map.130 = (bf16[128,768]{1,0:T(8,128)(2,1)}, bf16[128,256]{1,0:T(8,128)(2,1)}, bf16[128,256]{1,0:T(8,128)(2,1)}, bf16[128,256]{1,0:T(8,128)(2,1)}) custom-call(bf16[128,768]{1,0:T(8,128)(2,1)} %get-tuple-element.8.refs_0_, bf16[128,256]{1,0:T(8,128)(2,1)} %get-tuple-element.9.refs_1_, bf16[128,256]{1,0:T(8,128)(2,1)} %get-tuple-element.10.refs_2_, ...), custom_call_target="tpu_custom_call" | custom-call | tf_op jit(solution)/shard_map/pallas_call | solution.py:337

commit v5 on v4

--- a/solution.py
+++ b/solution.py
@@ -12,7 +12,7 @@
 F32 = jnp.float32
 BF16 = jnp.bfloat16
 ROWS = 16
-VMEM_BYTES = 63 * 1024 * 1024
+VMEM_BYTES = 32 * 1024 * 1024
 
 
 def iota(shape, dim):
@@ -30,12 +30,12 @@
 def kernel(
     n, pad, scaling,
     og_hbm, expert_hbm, counts_hbm, up_hbm, down_hbm, pre_hbm, q_hbm, k_hbm, v_hbm, wout_hbm,
-    gh_out, gq_out, gk_out, gv_out,
+    gh, gq, gk, gv,
     expert_of, counts, up, down, pre, wout, q, k, v, mask, grad_t, xsend, x, hsum,
-    ysend, yrecv, rsend, ret, eg, eg_in, gh, ks_send, ks_recv, ks, qs_send, qs_recv, qs,
-    gq, gk, gv,
+    ysend, yrecv, rsend, ret, part, part_in, grads, wall, head_send, head_recv,
+    ks_send, ks_recv, ks, qs_send, qs_recv, qs,
     load_sem, one_send, one_recv, disp_send, disp_recv, ax_send, ax_recv,
-    hy_send, hy_recv, ret_send, ret_recv, st_send, st_recv, out_sem,
+    hy_send, hy_recv, ret_send, ret_recv, st_send, st_recv, wall_send, wall_recv, head_ssem, head_rsem,
 ):
     s = lax.axis_index("seq")
     h = lax.axis_index("head")
@@ -43,6 +43,7 @@
     y = lax.div(h, 2)
     sib = (s, h + 1 - 2 * c)
     far = (s, lax.rem(h + 2, 4))
+    diag = (s, lax.rem(sib[1] + 2, 4))
     m = n // 2
     width, tok = og_hbm.shape
     pair = 2 * width
@@ -64,7 +65,7 @@
     peers = [lax.rem(s + d, n) for d in range(1, n)]
     for p in peers:
         pl.semaphore_signal(barrier, inc=1, device_id=(p, h), device_id_type=MESH)
-    for to in (sib, far):
+    for to in (sib, far, diag):
         pl.semaphore_signal(barrier, inc=1, device_id=to, device_id_type=MESH)
     loads = {}
     for i, (name, src, dst) in enumerate((
@@ -77,7 +78,7 @@
         loads[name] = pltpu.make_async_copy(src, dst, load_sem.at[i])
         loads[name].start()
 
-    pl.semaphore_wait(barrier, n + 1)
+    pl.semaphore_wait(barrier, n + 2)
     pending = []
 
     def start(copy):
@@ -92,6 +93,11 @@
     for i, (name, both) in enumerate((("pre", pre), ("down", down), ("up", up))):
         loads[name].wait()
         swaps.append(start(send(both.at[0], both.at[1], one_send.at[3 + i], one_recv.at[3 + i], sib)))
+
+    loads["wout"].wait()
+    wall[h] = wout[:, mine]
+    start(send(wout.at[:, other], wall.at[h], wall_send.at[0], wall_recv.at[0], far))
+    start(send(wout.at[:, mine], wall.at[h], wall_send.at[1], wall_recv.at[1], sib))
 
     loads["expert"].wait()
     e_row = expert_of[...]
@@ -133,7 +139,8 @@
     unpack = (iota((rows, pre.shape[1]), 1) == packed).astype(BF16)
     mask[0] = nn(unpack, pre[0]).astype(BF16)
 
-    for j, p in order:
+    near = [(j, lax.rem(s + c + 2 * j, n)) for j in sorted(range(m), key=lambda j: min(j, m - j))]
+    for j, p in near:
         i = lax.div(p, 2)
         spot = x.at[i, :, mine]
         copy = send(spot, spot, disp_send.at[j], disp_recv.at[i], (p, h))
@@ -142,6 +149,10 @@
         else:
             copy.wait_recv()
         start(send(spot, spot, ax_send.at[j], ax_recv.at[j], far))
+
+    spot = wall.at[far[1]]
+    send(spot, spot, wall_send.at[0], wall_recv.at[0], far).wait_recv()
+    start(send(spot, spot, wall_send.at[2], wall_recv.at[2], sib))
 
     loads["k"].wait()
     loads["v"].wait()
@@ -178,7 +189,7 @@
     ready = x[:, :, mine].reshape(rows, pair)
     middle = [nt(ready, down[u, :, mine]) for u in range(2)]
     swaps[2].wait_recv()
-    for j, p in order:
+    for j, p in near:
         spot = x.at[lax.div(p, 2), :, other]
         send(spot, spot, ax_send.at[j], ax_recv.at[j], far).wait_recv()
     ready = x[:, :, other].reshape(rows, pair)
@@ -216,57 +227,54 @@
     live_col = lax.rem(e_col, 2) == parity
     slot_col = jnp.where(live_col, lax.div(e_col, 2) * pad + rank_col, -1)
     combine = (iota((tok, rows), 1) == slot_col).astype(BF16)
-    own = grad_t[...].astype(F32).T
-    loads["wout"].wait()
+    own = jnp.where(live_col, grad_t[...].astype(F32).T, 0.0)
     loads["q"].wait()
     q_t = q[...].T
-    for j, p in order:
+    spot = wall.at[sib[1]]
+    send(spot, spot, wall_send.at[1], wall_recv.at[1], sib).wait_recv()
+    spot = wall.at[diag[1]]
+    send(spot, spot, wall_send.at[2], wall_recv.at[2], sib).wait_recv()
+    state_wait(1, ks)
+    for j, p in near:
         i = lax.div(p, 2)
         copy = send(ret.at[i], ret.at[i], ret_send.at[j], ret_recv.at[i], (p, h))
         if j == 0:
             pl.when(c == 1)(copy.wait_recv)
         else:
             copy.wait_recv()
-    share = nn(combine, ret[...].reshape(rows, pair))
-    eg[...] = share.astype(BF16)
-    start(send(eg, eg_in, one_send.at[1], one_recv.at[1], sib))
-    own = own + share
-    send(eg, eg_in, one_send.at[1], one_recv.at[1], sib).wait_recv()
-    half = (own + eg_in[...].astype(F32)).astype(BF16)
-    gh[:, mine] = half
-    spot = gh.at[:, mine]
-    start(send(spot, spot, one_send.at[2], one_recv.at[2], far))
-    head_part = nt(half, wout[:, mine])
-    state_wait(1, ks)
-    spot = gh.at[:, other]
-    send(spot, spot, one_send.at[2], one_recv.at[2], far).wait_recv()
-    head_grad = (head_part + nt(gh[:, other], wout[:, other])).astype(BF16)
+    half = (own + nn(combine, ret[...].reshape(rows, pair))).astype(BF16)
+    for i, to in enumerate((diag, far, sib)):
+        head_send[i] = nt(half, wall[to[1]]).astype(BF16)
+        start(send(head_send.at[i], head_recv.at[i], head_ssem.at[i], head_rsem.at[i], to))
+    part[...] = half
+    start(send(part, part_in, one_send.at[1], one_recv.at[1], sib))
+    head_sum = nt(half, wall[h])
+    for i, to in ((2, sib), (1, far), (0, diag)):
+        spot = head_recv.at[i]
+        send(spot, spot, head_ssem.at[i], head_rsem.at[i], to).wait_recv()
+        head_sum = head_sum + head_recv[i].astype(F32)
+    head_grad = head_sum.astype(BF16)
     qs_part = nn(q_t, head_grad).astype(BF16)
     for p in range(n):
         qs_send[p] = qs_part[p * piece : (p + 1) * piece]
     state_scatter(2, qs_send, qs_recv)
-    writes = []
-
-    def write(src, dst):
-        writes.append(pltpu.make_async_copy(src, dst, out_sem.at[len(writes)]))
-        writes[-1].start()
-
-    write(gh, gh_out)
+    send(part, part_in, one_send.at[1], one_recv.at[1], sib).wait_recv()
+    grads[:, mine] = part[...] + part_in[...]
+    spot = grads.at[:, mine]
+    start(send(spot, spot, one_send.at[2], one_recv.at[2], far))
     dim = n * piece
     gq[...] = (scaling * nt(head_grad, ks[...].reshape(dim, dim))).astype(BF16)
-    write(gq, gq_out)
     state_sum(2, qs_recv, qs)
+    spot = grads.at[:, other]
+    send(spot, spot, one_send.at[2], one_recv.at[2], far).wait_recv()
+    gh[...] = grads[...]
     state_wait(3, qs)
     q_round = qs[...].reshape(dim, dim)
     gk[...] = (scaling * nt(v[...], q_round)).astype(BF16)
-    write(gk, gk_out)
     gv[...] = (scaling * nn(k[...], q_round)).astype(BF16)
-    write(gv, gv_out)
 
     for copy in pending:
         copy.wait_send()
-    for copy in writes:
-        copy.wait()
 
     @pl.when(c == 1)
     def _():
@@ -275,15 +283,12 @@
 
 
 def write_out(*refs):
-    sources, dests, rooms, (come, go) = refs[:4], refs[4:8], refs[8:12], refs[12:]
-    ins = [pltpu.make_async_copy(a, b, come.at[i]) for i, (a, b) in enumerate(zip(sources, rooms))]
-    outs = [pltpu.make_async_copy(a, b, go.at[i]) for i, (a, b) in enumerate(zip(rooms, dests))]
-    for copy in ins:
+    count = len(refs) // 2
+    sem = refs[-1]
+    copies = [pltpu.make_async_copy(refs[i], refs[count + i], sem.at[i]) for i in range(count)]
+    for copy in copies:
         copy.start()
-    for first, second in zip(ins, outs):
-        first.wait()
-        second.start()
-    for copy in outs:
+    for copy in copies:
         copy.wait()
 
 
@@ -301,7 +306,7 @@
     piece = dim // n
     scaling = 1.0 / math.sqrt(dim * tok * n)
     hbm = pl.BlockSpec(memory_space=pltpu.HBM)
-    anywhere = pl.BlockSpec(memory_space=pl.ANY)
+    vmem = pl.BlockSpec(memory_space=pltpu.VMEM)
     dma = pltpu.SemaphoreType.DMA
 
     def buf(*shape, dtype=BF16):
@@ -314,7 +319,7 @@
         functools.partial(kernel, n, pad, scaling),
         out_shape=outs,
         in_specs=[hbm] * 10,
-        out_specs=(anywhere,) * 4,
+        out_specs=(vmem,) * 4,
         scratch_shapes=[
             buf(1, tok, dtype=jnp.int32), buf(1, n, dtype=jnp.int32),
             buf(2, depth, hidden), buf(2, hidden, depth), buf(2, slots, hidden), buf(dim, depth),
@@ -322,10 +327,11 @@
             buf(pair, tok), buf(m, pad, pair), buf(m, pad, depth), buf(m, pad, pair, dtype=F32),
             buf(m, pad, pair), buf(m, pad, pair), buf(m, pad, pair), buf(m, pad, pair),
             buf(tok, pair), buf(tok, pair), buf(tok, depth),
+            buf(4, dim, pair), buf(3, tok, dim), buf(3, tok, dim),
             state, state, state, state, state, state,
-            buf(tok, dim), buf(tok, dim), buf(tok, dim),
             dma((10,)), dma((6,)), dma((6,)), dma((m,)), dma((m,)), dma((m,)), dma((m,)),
-            dma((m,)), dma((m,)), dma((m,)), dma((m,)), dma((4, n)), dma((4, n)), dma((4,)),
+            dma((m,)), dma((m,)), dma((m,)), dma((m,)), dma((4, n)), dma((4, n)), dma((3,)), dma((3,)),
+            dma((3,)), dma((3,)),
         ],
         compiler_params=pltpu.CompilerParams(
             collective_id=0, has_side_effects=True, vmem_limit_bytes=VMEM_BYTES
@@ -337,10 +343,10 @@
     return pl.pallas_call(
         write_out,
         out_shape=outs,
-        in_specs=[anywhere] * 4,
+        in_specs=[vmem] * 4,
         out_specs=(hbm,) * 4,
-        scratch_shapes=[*(buf(*a.shape) for a in outs), dma((4,)), dma((4,))],
-        compiler_params=pltpu.CompilerParams(vmem_limit_bytes=VMEM_BYTES),
+        scratch_shapes=[dma((4,))],
+        compiler_params=pltpu.CompilerParams(vmem_limit_bytes=VMEM_BYTES // 8),
     )(*results)
 
 

time: 45.6 us -> 43.9 us (0.963)
  Pallas kernels: 44.8 us -> 43.1 us
    pallas_call x1, Pallas kernels: 1.73 us -> 0.77 us  [fused(): pl.pallas_call(write_out, out_shape=outs, in_specs=[vmem] * 4, out_specs=...]
    pallas_call x1, Pallas kernels: 43 us -> 42.3 us  [fused(): pl.pallas_call(functools.partial(kernel, n, pad, scaling), out_shape=outs...]
where the time goes in v5:
time: 43.9 us; the launch traced here: 43.7 us
  Pallas kernels  43.1 us (98%)
  between operations  0.64 us (1%)
    pallas_call x1, Pallas kernels, fused(): pl.pallas_call(functools.partial(kernel, n, pad, scaling), out_shape=outs...  42.3 us

profile of v5, /device:TPU:0, one launch (start us, length us, event | category | flops | bytes accessed | tf_op | source)
XLA Modules:
  0.0 43.7 jit_solution(2502429521869968926)
XLA Ops:
  0.6 42.3 %shard_map.129 = (bf16[128,768]{1,0:T(8,128)(2,1)S(1)}, bf16[128,256]{1,0:T(8,128)(2,1)S(1)}, bf16[128,256]{1,0:T(8,128)(2,1)S(1)}, bf16[128,256]{1,0:T(8,128)(2,1)S(1)}) custom-call(bf16[192,128]{1,0:T(8,128)(2,1)} %bitcast.3, s32[1,128]{1,0:T(1,128)} %bitcast.4, s32[1,8]{1,0:T(1,128)} %bitcast.5, bf16[1,768,768]{2,1,0:T(8,128)(2,1)} %up_hbm.1, ...), custom_call_target="tpu_custom_call" | custom-call | tf_op jit(solution)/shard_map/pallas_call | solution.py:318
  42.9 0.8 %shard_map.130 = (bf16[128,768]{1,0:T(8,128)(2,1)}, bf16[128,256]{1,0:T(8,128)(2,1)}, bf16[128,256]{1,0:T(8,128)(2,1)}, bf16[128,256]{1,0:T(8,128)(2,1)}) custom-call(bf16[128,768]{1,0:T(8,128)(2,1)S(1)} %get-tuple-element.8.refs_0_, bf16[128,256]{1,0:T(8,128)(2,1)S(1)} %get-tuple-element.9.refs_1_, bf16[128,256]{1,0:T(8,128)(2,1)S(1)} %get-tuple-element.10.refs_2_, ...), custom_call_target="tpu_custom_call" | custom-call | tf_op jit(solution)/shard_map/pallas_call | solution.py:343

commit v6 on v5

--- a/solution.py
+++ b/solution.py
@@ -89,16 +89,6 @@
     loads["grad"].wait()
     spot = grad_t.at[own_rows]
     start(send(spot, spot, one_send.at[0], one_recv.at[0], sib))
-    swaps = []
-    for i, (name, both) in enumerate((("pre", pre), ("down", down), ("up", up))):
-        loads[name].wait()
-        swaps.append(start(send(both.at[0], both.at[1], one_send.at[3 + i], one_recv.at[3 + i], sib)))
-
-    loads["wout"].wait()
-    wall[h] = wout[:, mine]
-    start(send(wout.at[:, other], wall.at[h], wall_send.at[0], wall_recv.at[0], far))
-    start(send(wout.at[:, mine], wall.at[h], wall_send.at[1], wall_recv.at[1], sib))
-
     loads["expert"].wait()
     e_row = expert_of[...]
     eye = iota((tok, tok), 0) == iota((tok, tok), 1)
@@ -109,6 +99,16 @@
     live_row = lax.rem(e_row, 2) == parity
     slot_row = jnp.where(live_row, lax.div(e_row, 2) * pad + rank_row, -1)
     scatter = (iota((rows, tok), 0) == slot_row).astype(BF16)
+
+    swaps = []
+    for i, (name, both) in enumerate((("pre", pre), ("down", down), ("up", up))):
+        loads[name].wait()
+        swaps.append(start(send(both.at[0], both.at[1], one_send.at[3 + i], one_recv.at[3 + i], sib)))
+
+    loads["wout"].wait()
+    wall[h] = wout[:, mine]
+    start(send(wout.at[:, other], wall.at[h], wall_send.at[0], wall_recv.at[0], far))
+    start(send(wout.at[:, mine], wall.at[h], wall_send.at[1], wall_recv.at[1], sib))
 
     spot = grad_t.at[sib_rows]
     send(spot, spot, one_send.at[0], one_recv.at[0], sib).wait_recv()
@@ -137,7 +137,7 @@
     before = iota((rows, n), 1) < source
     packed = jnp.sum(jnp.where(before, counts[...], 0), axis=1, keepdims=True) + lax.rem(slot, pad)
     unpack = (iota((rows, pre.shape[1]), 1) == packed).astype(BF16)
-    mask[0] = nn(unpack, pre[0]).astype(BF16)
+    mask[0] = nn(unpack, pre[0]).astype(BF16).reshape(m, pad, -1)
 
     near = [(j, lax.rem(s + c + 2 * j, n)) for j in sorted(range(m), key=lambda j: min(j, m - j))]
     for j, p in near:
@@ -184,29 +184,36 @@
     state_scatter(0, ks_send, ks_recv)
 
     swaps[0].wait_recv()
-    mask[1] = nn(unpack, pre[1]).astype(BF16)
+    mask[1] = nn(unpack, pre[1]).astype(BF16).reshape(m, pad, -1)
     swaps[1].wait_recv()
-    ready = x[:, :, mine].reshape(rows, pair)
-    middle = [nt(ready, down[u, :, mine]) for u in range(2)]
     swaps[2].wait_recv()
+    group = max(m // 2, 1)
+    mids = []
+    for g in range(0, m, group):
+        some = [(j, lax.div(p, 2)) for j, p in near[g : g + group]]
+        ready = jnp.concatenate([x[i, :, mine] for _, i in some], axis=0)
+        middle = [nt(ready, down[u, :, mine]) for u in range(2)]
+        for j, i in some:
+            spot = x.at[i, :, other]
+            send(spot, spot, ax_send.at[j], ax_recv.at[j], far).wait_recv()
+        ready = jnp.concatenate([x[i, :, other] for _, i in some], axis=0)
+        mid = []
+        for u in range(2):
+            full_sum = middle[u] + nt(ready, down[u, :, other])
+            live = jnp.concatenate([mask[u, i] for _, i in some], axis=0)
+            mid.append(jnp.where(live > 0, full_sum, 0.0).astype(BF16))
+        away = (nt(mid[0], up[0, other, :]) + nt(mid[1], up[1, other, :])).astype(BF16)
+        for at, (j, i) in enumerate(some):
+            ysend[i] = away[at * pad : (at + 1) * pad]
+            start(send(ysend.at[i], yrecv.at[i], hy_send.at[j], hy_recv.at[j], far))
+        mids.append((some, mid))
+    for some, mid in mids:
+        stay = nt(mid[0], up[0, mine, :]) + nt(mid[1], up[1, mine, :])
+        for at, (j, i) in enumerate(some):
+            hsum[i] = stay[at * pad : (at + 1) * pad]
+    state_sum(0, ks_recv, ks)
+
     for j, p in near:
-        spot = x.at[lax.div(p, 2), :, other]
-        send(spot, spot, ax_send.at[j], ax_recv.at[j], far).wait_recv()
-    ready = x[:, :, other].reshape(rows, pair)
-    mid = [
-        jnp.where(mask[u] > 0, middle[u] + nt(ready, down[u, :, other]), 0.0).astype(BF16)
-        for u in range(2)
-    ]
-    ysend[...] = (nt(mid[0], up[0, other, :]) + nt(mid[1], up[1, other, :])).astype(BF16).reshape(
-        m, pad, pair
-    )
-    for j, p in order:
-        i = lax.div(p, 2)
-        start(send(ysend.at[i], yrecv.at[i], hy_send.at[j], hy_recv.at[j], far))
-    hsum[...] = (nt(mid[0], up[0, mine, :]) + nt(mid[1], up[1, mine, :])).reshape(m, pad, pair)
-    state_sum(0, ks_recv, ks)
-
-    for j, p in order:
         i = lax.div(p, 2)
         spot = yrecv.at[i]
         send(spot, spot, hy_send.at[j], hy_recv.at[j], far).wait_recv()
@@ -243,35 +250,48 @@
         else:
             copy.wait_recv()
     half = (own + nn(combine, ret[...].reshape(rows, pair))).astype(BF16)
-    for i, to in enumerate((diag, far, sib)):
-        head_send[i] = nt(half, wall[to[1]]).astype(BF16)
-        start(send(head_send.at[i], head_recv.at[i], head_ssem.at[i], head_rsem.at[i], to))
+    dim = n * piece
+    cut = dim // 2
+    for b in range(2):
+        for i, to in enumerate((diag, far, sib)):
+            head_send[b, i] = nt(half, wall[to[1], b * cut : (b + 1) * cut, :]).astype(BF16)
+            start(send(
+                head_send.at[b, i], head_recv.at[b, i], head_ssem.at[b, i], head_rsem.at[b, i], to
+            ))
     part[...] = half
     start(send(part, part_in, one_send.at[1], one_recv.at[1], sib))
-    head_sum = nt(half, wall[h])
-    for i, to in ((2, sib), (1, far), (0, diag)):
-        spot = head_recv.at[i]
-        send(spot, spot, head_ssem.at[i], head_rsem.at[i], to).wait_recv()
-        head_sum = head_sum + head_recv[i].astype(F32)
-    head_grad = head_sum.astype(BF16)
-    qs_part = nn(q_t, head_grad).astype(BF16)
-    for p in range(n):
-        qs_send[p] = qs_part[p * piece : (p + 1) * piece]
-    state_scatter(2, qs_send, qs_recv)
+    head_grad = []
+    for b in range(2):
+        head_sum = nt(half, wall[h, b * cut : (b + 1) * cut, :])
+        for i, to in ((2, sib), (1, far), (0, diag)):
+            spot = head_recv.at[b, i]
+            send(spot, spot, head_ssem.at[b, i], head_rsem.at[b, i], to).wait_recv()
+            head_sum = head_sum + head_recv[b, i].astype(F32)
+        head_grad.append(head_sum.astype(BF16))
+        qs_part = nn(q_t, head_grad[b]).astype(BF16)
+        for p in range(n):
+            qs_send[b, p] = qs_part[p * piece : (p + 1) * piece]
+        state_scatter(2 + 2 * b, qs_send.at[b], qs_recv.at[b])
     send(part, part_in, one_send.at[1], one_recv.at[1], sib).wait_recv()
     grads[:, mine] = part[...] + part_in[...]
     spot = grads.at[:, mine]
     start(send(spot, spot, one_send.at[2], one_recv.at[2], far))
-    dim = n * piece
-    gq[...] = (scaling * nt(head_grad, ks[...].reshape(dim, dim))).astype(BF16)
-    state_sum(2, qs_recv, qs)
+    k_round = ks[...].reshape(dim, dim)
+    gq[...] = (
+        scaling * (nt(head_grad[0], k_round[:, :cut]) + nt(head_grad[1], k_round[:, cut:]))
+    ).astype(BF16)
+    for b in range(2):
+        state_sum(2 + 2 * b, qs_recv.at[b], qs.at[b])
     spot = grads.at[:, other]
     send(spot, spot, one_send.at[2], one_recv.at[2], far).wait_recv()
     gh[...] = grads[...]
-    state_wait(3, qs)
-    q_round = qs[...].reshape(dim, dim)
-    gk[...] = (scaling * nt(v[...], q_round)).astype(BF16)
-    gv[...] = (scaling * nn(k[...], q_round)).astype(BF16)
+    key_sum = 0.0
+    for b in range(2):
+        state_wait(3 + 2 * b, qs.at[b])
+        q_round = qs[b].reshape(dim, cut)
+        gv[:, b * cut : (b + 1) * cut] = (scaling * nn(k[...], q_round)).astype(BF16)
+        key_sum = key_sum + nt(v[:, b * cut : (b + 1) * cut], q_round)
+    gk[...] = (scaling * key_sum).astype(BF16)
 
     for copy in pending:
         copy.wait_send()
@@ -313,6 +333,7 @@
         return pltpu.VMEM(shape, dtype)
 
     state = buf(n, piece, dim)
+    halves = buf(2, n, piece, dim // 2)
     out = jax.ShapeDtypeStruct((tok, dim), BF16)
     outs = (jax.ShapeDtypeStruct((tok, depth), BF16), out, out, out)
     results = pl.pallas_call(
@@ -323,15 +344,15 @@
         scratch_shapes=[
             buf(1, tok, dtype=jnp.int32), buf(1, n, dtype=jnp.int32),
             buf(2, depth, hidden), buf(2, hidden, depth), buf(2, slots, hidden), buf(dim, depth),
-            buf(tok, dim), buf(tok, dim), buf(tok, dim), buf(2, rows, hidden),
+            buf(tok, dim), buf(tok, dim), buf(tok, dim), buf(2, m, pad, hidden),
             buf(pair, tok), buf(m, pad, pair), buf(m, pad, depth), buf(m, pad, pair, dtype=F32),
             buf(m, pad, pair), buf(m, pad, pair), buf(m, pad, pair), buf(m, pad, pair),
             buf(tok, pair), buf(tok, pair), buf(tok, depth),
-            buf(4, dim, pair), buf(3, tok, dim), buf(3, tok, dim),
-            state, state, state, state, state, state,
+            buf(4, dim, pair), buf(2, 3, tok, dim // 2), buf(2, 3, tok, dim // 2),
+            state, state, state, halves, halves, halves,
             dma((10,)), dma((6,)), dma((6,)), dma((m,)), dma((m,)), dma((m,)), dma((m,)),
-            dma((m,)), dma((m,)), dma((m,)), dma((m,)), dma((4, n)), dma((4, n)), dma((3,)), dma((3,)),
-            dma((3,)), dma((3,)),
+            dma((m,)), dma((m,)), dma((m,)), dma((m,)), dma((6, n)), dma((6, n)), dma((3,)), dma((3,)),
+            dma((2, 3)), dma((2, 3)),
         ],
         compiler_params=pltpu.CompilerParams(
             collective_id=0, has_side_effects=True, vmem_limit_bytes=VMEM_BYTES
@@ -353,7 +374,7 @@
 def step(*arrays):
     n, heads = lax.axis_size("seq"), lax.axis_size("head")
     width, dim = arrays[0].shape[1], arrays[6].shape[1]
-    fits = heads == 4 and n % 2 == 0 and dim % (n * ROWS) == 0 and 2 * width % 128 == 0
+    fits = heads == 4 and n % 2 == 0 and dim % (n * ROWS) == 0 and dim % 256 == 0 and 2 * width % 128 == 0
     return (fused if fits else shards)(*arrays)
 
 

time: 43.9 us -> 42.9 us (0.977)
  Pallas kernels: 43.1 us -> 42.1 us
    pallas_call x1, Pallas kernels: 42.3 us -> 41.4 us  [fused(): pl.pallas_call(functools.partial(kernel, n, pad, scaling), out_shape=outs...]
where the time goes in v6:
time: 42.9 us; the launch traced here: 42.8 us
  Pallas kernels  42.1 us (98%)
  between operations  0.64 us (1%)
    pallas_call x1, Pallas kernels, fused(): pl.pallas_call(functools.partial(kernel, n, pad, scaling), out_shape=outs...  41.4 us

profile of v6, /device:TPU:0, one launch (start us, length us, event | category | flops | bytes accessed | tf_op | source)
XLA Modules:
  0.0 42.8 jit_solution(17079488418462386729)
XLA Ops:
  0.6 41.4 %shard_map.129 = (bf16[128,768]{1,0:T(8,128)(2,1)S(1)}, bf16[128,256]{1,0:T(8,128)(2,1)S(1)}, bf16[128,256]{1,0:T(8,128)(2,1)S(1)}, bf16[128,256]{1,0:T(8,128)(2,1)S(1)}) custom-call(bf16[192,128]{1,0:T(8,128)(2,1)} %bitcast.3, s32[1,128]{1,0:T(1,128)} %bitcast.4, s32[1,8]{1,0:T(1,128)} %bitcast.5, bf16[1,768,768]{2,1,0:T(8,128)(2,1)} %up_hbm.1, ...), custom_call_target="tpu_custom_call" | custom-call | tf_op jit(solution)/shard_map/pallas_call | solution.py:339
  42.0 0.8 %shard_map.130 = (bf16[128,768]{1,0:T(8,128)(2,1)}, bf16[128,256]{1,0:T(8,128)(2,1)}, bf16[128,256]{1,0:T(8,128)(2,1)}, bf16[128,256]{1,0:T(8,128)(2,1)}) custom-call(bf16[128,768]{1,0:T(8,128)(2,1)S(1)} %get-tuple-element.8.refs_0_, bf16[128,256]{1,0:T(8,128)(2,1)S(1)} %get-tuple-element.9.refs_1_, bf16[128,256]{1,0:T(8,128)(2,1)S(1)} %get-tuple-element.10.refs_2_, ...), custom_call_target="tpu_custom_call" | custom-call | tf_op jit(solution)/shard_map/pallas_call | solution.py:364

commit v7 on v6

--- a/solution.py
+++ b/solution.py
@@ -70,9 +70,9 @@
     loads = {}
     for i, (name, src, dst) in enumerate((
         ("expert", expert_hbm, expert_of), ("grad", og_hbm, grad_t.at[own_rows]),
-        ("k", k_hbm, k), ("v", v_hbm, v), ("counts", counts_hbm, counts),
+        ("wout", wout_hbm, wout), ("k", k_hbm, k), ("v", v_hbm, v), ("counts", counts_hbm, counts),
         ("pre", pre_hbm, pre.at[0]), ("down", down_hbm.at[0], down.at[0]),
-        ("up", up_hbm.at[0], up.at[0]), ("wout", wout_hbm, wout),
+        ("up", up_hbm.at[0], up.at[0]),
         ("q", q_hbm, q),
     )):
         loads[name] = pltpu.make_async_copy(src, dst, load_sem.at[i])
@@ -89,6 +89,25 @@
     loads["grad"].wait()
     spot = grad_t.at[own_rows]
     start(send(spot, spot, one_send.at[0], one_recv.at[0], sib))
+    cut = n * piece // 2
+
+    def wall_rows(k):
+        return pl.ds(k * cut, cut)
+
+    def wall_swap(k):
+        start(send(
+            wout.at[wall_rows(k), other], wall.at[h, wall_rows(k)],
+            wall_send.at[k], wall_recv.at[k], far,
+        ))
+
+    def wall_relay(k):
+        spot = wall.at[far[1], wall_rows(k)]
+        send(spot, spot, wall_send.at[k], wall_recv.at[k], far).wait_recv()
+        start(send(spot, spot, wall_send.at[3 + k], wall_recv.at[3 + k], sib))
+
+    loads["wout"].wait()
+    wall_swap(0)
+
     loads["expert"].wait()
     e_row = expert_of[...]
     eye = iota((tok, tok), 0) == iota((tok, tok), 1)
@@ -105,10 +124,8 @@
         loads[name].wait()
         swaps.append(start(send(both.at[0], both.at[1], one_send.at[3 + i], one_recv.at[3 + i], sib)))
 
-    loads["wout"].wait()
     wall[h] = wout[:, mine]
-    start(send(wout.at[:, other], wall.at[h], wall_send.at[0], wall_recv.at[0], far))
-    start(send(wout.at[:, mine], wall.at[h], wall_send.at[1], wall_recv.at[1], sib))
+    start(send(wout.at[:, mine], wall.at[h], wall_send.at[2], wall_recv.at[2], sib))
 
     spot = grad_t.at[sib_rows]
     send(spot, spot, one_send.at[0], one_recv.at[0], sib).wait_recv()
@@ -150,9 +167,7 @@
             copy.wait_recv()
         start(send(spot, spot, ax_send.at[j], ax_recv.at[j], far))
 
-    spot = wall.at[far[1]]
-    send(spot, spot, wall_send.at[0], wall_recv.at[0], far).wait_recv()
-    start(send(spot, spot, wall_send.at[2], wall_recv.at[2], sib))
+    wall_relay(0)
 
     loads["k"].wait()
     loads["v"].wait()
@@ -183,16 +198,20 @@
 
     state_scatter(0, ks_send, ks_recv)
 
+    group = max(m // 2, 1)
+    groups = [
+        [(j, lax.div(p, 2)) for j, p in near[g : g + group]] for g in range(0, m, group)
+    ]
+    firsts = [jnp.concatenate([x[i, :, mine] for _, i in some], axis=0) for some in groups]
+    middles = [[nt(ready, down[0, :, mine])] for ready in firsts]
     swaps[0].wait_recv()
     mask[1] = nn(unpack, pre[1]).astype(BF16).reshape(m, pad, -1)
     swaps[1].wait_recv()
+    for middle, ready in zip(middles, firsts):
+        middle.append(nt(ready, down[1, :, mine]))
     swaps[2].wait_recv()
-    group = max(m // 2, 1)
     mids = []
-    for g in range(0, m, group):
-        some = [(j, lax.div(p, 2)) for j, p in near[g : g + group]]
-        ready = jnp.concatenate([x[i, :, mine] for _, i in some], axis=0)
-        middle = [nt(ready, down[u, :, mine]) for u in range(2)]
+    for some, middle in zip(groups, middles):
         for j, i in some:
             spot = x.at[i, :, other]
             send(spot, spot, ax_send.at[j], ax_recv.at[j], far).wait_recv()
@@ -207,6 +226,7 @@
             ysend[i] = away[at * pad : (at + 1) * pad]
             start(send(ysend.at[i], yrecv.at[i], hy_send.at[j], hy_recv.at[j], far))
         mids.append((some, mid))
+    wall_swap(1)
     for some, mid in mids:
         stay = nt(mid[0], up[0, mine, :]) + nt(mid[1], up[1, mine, :])
         for at, (j, i) in enumerate(some):
@@ -237,10 +257,12 @@
     own = jnp.where(live_col, grad_t[...].astype(F32).T, 0.0)
     loads["q"].wait()
     q_t = q[...].T
+    wall_relay(1)
     spot = wall.at[sib[1]]
-    send(spot, spot, wall_send.at[1], wall_recv.at[1], sib).wait_recv()
-    spot = wall.at[diag[1]]
     send(spot, spot, wall_send.at[2], wall_recv.at[2], sib).wait_recv()
+    for b in range(2):
+        spot = wall.at[diag[1], wall_rows(b)]
+        send(spot, spot, wall_send.at[3 + b], wall_recv.at[3 + b], sib).wait_recv()
     state_wait(1, ks)
     for j, p in near:
         i = lax.div(p, 2)
@@ -251,7 +273,6 @@
             copy.wait_recv()
     half = (own + nn(combine, ret[...].reshape(rows, pair))).astype(BF16)
     dim = n * piece
-    cut = dim // 2
     for b in range(2):
         for i, to in enumerate((diag, far, sib)):
             head_send[b, i] = nt(half, wall[to[1], b * cut : (b + 1) * cut, :]).astype(BF16)
@@ -351,7 +372,7 @@
             buf(4, dim, pair), buf(2, 3, tok, dim // 2), buf(2, 3, tok, dim // 2),
             state, state, state, halves, halves, halves,
             dma((10,)), dma((6,)), dma((6,)), dma((m,)), dma((m,)), dma((m,)), dma((m,)),
-            dma((m,)), dma((m,)), dma((m,)), dma((m,)), dma((6, n)), dma((6, n)), dma((3,)), dma((3,)),
+            dma((m,)), dma((m,)), dma((m,)), dma((m,)), dma((6, n)), dma((6, n)), dma((5,)), dma((5,)),
             dma((2, 3)), dma((2, 3)),
         ],
         compiler_params=pltpu.CompilerParams(

time: 42.9 us -> 43 us (level)
  no operation moved by 1% of the time
where the time goes in v7:
time: 43 us; the launch traced here: 42.8 us
  Pallas kernels  42.2 us (98%)
  between operations  0.64 us (1%)
    pallas_call x1, Pallas kernels, fused(): pl.pallas_call(functools.partial(kernel, n, pad, scaling), out_shape=outs...  41.4 us

profile of v7, /device:TPU:0, one launch (start us, length us, event | category | flops | bytes accessed | tf_op | source)
XLA Modules:
  0.0 42.8 jit_solution(12678282384853031201)
XLA Ops:
  0.6 41.4 %shard_map.129 = (bf16[128,768]{1,0:T(8,128)(2,1)S(1)}, bf16[128,256]{1,0:T(8,128)(2,1)S(1)}, bf16[128,256]{1,0:T(8,128)(2,1)S(1)}, bf16[128,256]{1,0:T(8,128)(2,1)S(1)}) custom-call(bf16[192,128]{1,0:T(8,128)(2,1)} %bitcast.3, s32[1,128]{1,0:T(1,128)} %bitcast.4, s32[1,8]{1,0:T(1,128)} %bitcast.5, bf16[1,768,768]{2,1,0:T(8,128)(2,1)} %up_hbm.1, ...), custom_call_target="tpu_custom_call" | custom-call | tf_op jit(solution)/shard_map/pallas_call | solution.py:360
  42.0 0.8 %shard_map.130 = (bf16[128,768]{1,0:T(8,128)(2,1)}, bf16[128,256]{1,0:T(8,128)(2,1)}, bf16[128,256]{1,0:T(8,128)(2,1)}, bf16[128,256]{1,0:T(8,128)(2,1)}) custom-call(bf16[128,768]{1,0:T(8,128)(2,1)S(1)} %get-tuple-element.8.refs_0_, bf16[128,256]{1,0:T(8,128)(2,1)S(1)} %get-tuple-element.9.refs_1_, bf16[128,256]{1,0:T(8,128)(2,1)S(1)} %get-tuple-element.10.refs_2_, ...), custom_call_target="tpu_custom_call" | custom-call | tf_op jit(solution)/shard_map/pallas_call | solution.py:385

commit v8 on v7

--- a/solution.py
+++ b/solution.py
@@ -226,12 +226,13 @@
             ysend[i] = away[at * pad : (at + 1) * pad]
             start(send(ysend.at[i], yrecv.at[i], hy_send.at[j], hy_recv.at[j], far))
         mids.append((some, mid))
+        if len(mids) == 1:
+            state_sum(0, ks_recv, ks)
     wall_swap(1)
     for some, mid in mids:
         stay = nt(mid[0], up[0, mine, :]) + nt(mid[1], up[1, mine, :])
         for at, (j, i) in enumerate(some):
             hsum[i] = stay[at * pad : (at + 1) * pad]
-    state_sum(0, ks_recv, ks)
 
     for j, p in near:
         i = lax.div(p, 2)
@@ -263,7 +264,6 @@
     for b in range(2):
         spot = wall.at[diag[1], wall_rows(b)]
         send(spot, spot, wall_send.at[3 + b], wall_recv.at[3 + b], sib).wait_recv()
-    state_wait(1, ks)
     for j, p in near:
         i = lax.div(p, 2)
         copy = send(ret.at[i], ret.at[i], ret_send.at[j], ret_recv.at[i], (p, h))
@@ -297,6 +297,7 @@
     grads[:, mine] = part[...] + part_in[...]
     spot = grads.at[:, mine]
     start(send(spot, spot, one_send.at[2], one_recv.at[2], far))
+    state_wait(1, ks)
     k_round = ks[...].reshape(dim, dim)
     gq[...] = (
         scaling * (nt(head_grad[0], k_round[:, :cut]) + nt(head_grad[1], k_round[:, cut:]))

time: 43 us -> 42.6 us (level)
  no operation moved by 1% of the time
where the time goes in v8:
time: 42.6 us; the launch traced here: 42.5 us
  Pallas kernels  41.8 us (98%)
  between operations  0.64 us (2%)
    pallas_call x1, Pallas kernels, fused(): pl.pallas_call(functools.partial(kernel, n, pad, scaling), out_shape=outs...  41 us

profile of v8, /device:TPU:0, one launch (start us, length us, event | category | flops | bytes accessed | tf_op | source)
XLA Modules:
  0.0 42.5 jit_solution(2422570915278686798)
XLA Ops:
  0.6 41.0 %shard_map.129 = (bf16[128,768]{1,0:T(8,128)(2,1)S(1)}, bf16[128,256]{1,0:T(8,128)(2,1)S(1)}, bf16[128,256]{1,0:T(8,128)(2,1)S(1)}, bf16[128,256]{1,0:T(8,128)(2,1)S(1)}) custom-call(bf16[192,128]{1,0:T(8,128)(2,1)} %bitcast.3, s32[1,128]{1,0:T(1,128)} %bitcast.4, s32[1,8]{1,0:T(1,128)} %bitcast.5, bf16[1,768,768]{2,1,0:T(8,128)(2,1)} %up_hbm.1, ...), custom_call_target="tpu_custom_call" | custom-call | tf_op jit(solution)/shard_map/pallas_call | solution.py:361
  41.7 0.8 %shard_map.130 = (bf16[128,768]{1,0:T(8,128)(2,1)}, bf16[128,256]{1,0:T(8,128)(2,1)}, bf16[128,256]{1,0:T(8,128)(2,1)}, bf16[128,256]{1,0:T(8,128)(2,1)}) custom-call(bf16[128,768]{1,0:T(8,128)(2,1)S(1)} %get-tuple-element.8.refs_0_, bf16[128,256]{1,0:T(8,128)(2,1)S(1)} %get-tuple-element.9.refs_1_, bf16[128,256]{1,0:T(8,128)(2,1)S(1)} %get-tuple-element.10.refs_2_, ...), custom_call_target="tpu_custom_call" | custom-call | tf_op jit(solution)/shard_map/pallas_call | solution.py:386
